TPU v7x, 32 devices: a whole 2x2x4 slice. The times are simulated.
32 devices in a mesh: wide: 8 (over z, x), narrow: 4 (over y, core).
Axes of the slice: x: 2, y: 2, z: 4, core: 2. Of those that a mesh axis runs over, the one named last changes fastest.
Arguments:
- table: bfloat16 [6291456, 16], P(('wide', 'narrow')), may hold values from -6 to 6
- dense: float32 [16384, 16], P(('wide', 'narrow')), may hold values from -400 to 400
- domains: int32 [16384], P(('wide', 'narrow')), may hold values from 0 to 1, as said below
- lengths: int32 [32, 512], P(('wide', 'narrow')), may hold values from 1 to 200, 32768 in all within a row
- requests: int32 [32, 32, 256], P(('wide', 'narrow')), may hold values from 0 to 196607, as said below
- counts: int32 [32, 32], P(('wide', 'narrow')), may hold values from 64 to 256
- field_slots: int32 [16384, 38], P(('wide', 'narrow')), may hold values from 0 to 8191, as said below
- behave_slots: int32 [32, 32768], P(('wide', 'narrow')), may hold values from 0 to 8191, as said below
- proj_w: bfloat16 [640, 512], replicated, may hold values from -0.25 to 0.25
- proj_b: float32 [512], replicated, may hold values from -3 to 3
- inter_gain: float32 [512], replicated, may hold values from 0.5 to 1.5
- inter_bias: float32 [512], replicated, may hold values from -3 to 3
- w_in: bfloat16 [4, 512, 1024], replicated, may hold values from -0.25 to 0.25
- b_in: float32 [4, 1024], replicated, may hold values from -3 to 3
- w_out: bfloat16 [4, 1024, 512], replicated, may hold values from -0.1875 to 0.1875
- b_out: float32 [4, 512], replicated, may hold values from -3 to 3
- expert_gain: float32 [4, 512], replicated, may hold values from 0.5 to 1.5
- expert_bias: float32 [4, 512], replicated, may hold values from -3 to 3
- shared_gate: bfloat16 [512, 2], replicated, may hold values from -0.25 to 0.25
- group_gate: bfloat16 [2, 512, 2], replicated, may hold values from -0.25 to 0.25
- tower_in: bfloat16 [2, 512, 256], replicated, may hold values from -0.25 to 0.25
- tower_in_bias: float32 [2, 256], replicated, may hold values from -3 to 3
- tower_out: float32 [2, 256], replicated, may hold values from -0.375 to 0.375
- tower_out_bias: float32 [2], replicated, may hold values from -3 to 3
- pred_cotangent: float32 [16384], P(('wide', 'narrow')), may hold values from -6 to 6
Outputs:
- pred: float32 [16384], P(('wide', 'narrow'))
- dense_grad: float32 [16384, 16], P(('wide', 'narrow'))
- table_grad: float32 [6291456, 16], P(('wide', 'narrow'))
- proj_w_grad: float32 [640, 512], replicated
- proj_b_grad: float32 [512], replicated
- inter_gain_grad: float32 [512], replicated
- inter_bias_grad: float32 [512], replicated
- w_in_grad: float32 [4, 512, 1024], replicated
- b_in_grad: float32 [4, 1024], replicated
- w_out_grad: float32 [4, 1024, 512], replicated
- b_out_grad: float32 [4, 512], replicated
- expert_gain_grad: float32 [4, 512], replicated
- expert_bias_grad: float32 [4, 512], replicated
- shared_gate_grad: float32 [512, 2], replicated
- group_gate_grad: float32 [2, 512, 2], replicated
- tower_in_grad: float32 [2, 512, 256], replicated
- tower_in_bias_grad: float32 [2, 256], replicated
- tower_out_grad: float32 [2, 256], replicated
- tower_out_bias_grad: float32 [2], replicated
Inputs may be any that keep to these rules, and one draw needn't show every extreme that they name: Within one block of 256 requests from one device to one owner the rows are distinct; slots at or past the block's count are padding. `field_slots`: each entry is o * 256 + j for an owner o and a live slot j of the event's device. `behave_slots`: each entry is o * 256 + j for an owner o and a live slot j of that device. `domains`: every device holds events of every domain. Each device's lengths sum to 32768.
All inputs are finite; a program needn't handle non-finite values.
Results may differ from a plain program's by a relative error of at most 0.011.
Values may be sent and summed in bfloat16 or wider, within the bound.
A program may use at most 320 MiB of HBM per device.

v0:
```python
import functools
import math

import jax
import jax.numpy as jnp
from jax import lax
from jax.experimental import pallas as pl
from jax.experimental.pallas import tpu as pltpu
from jax.sharding import PartitionSpec as P

SHARED = 2
DOMAINS = 2

EPSILON = 1e-05

f32 = jnp.float32
bf16 = jnp.bfloat16
i32 = jnp.int32
MESH = pl.DeviceIdType.MESH
AXES = ("wide", "narrow")
NT = (((1,), (1,)), ((), ()))
TN = (((0,), (0,)), ((), ()))
VMEM_LIMIT = 60 * 1024 * 1024
ROW_CHUNK = 1024
GROUP = 8
SPAN = 6


def vmem():
    return pl.BlockSpec(memory_space=pltpu.VMEM)


def smem():
    return pl.BlockSpec(memory_space=pltpu.SMEM)


def hbm():
    return pl.BlockSpec(memory_space=pl.ANY)


def params(**more):
    return pltpu.CompilerParams(vmem_limit_bytes=VMEM_LIMIT, **more)


def line_of(rows):
    return jnp.left_shift(jnp.right_shift(rows, 10), 7) + jnp.bitwise_and(rows, 127)


def lane_group_of(rows):
    return jnp.bitwise_and(jnp.right_shift(rows, 7), 7)


def identity(n):
    return (lax.broadcasted_iota(i32, (n, n), 0) == lax.broadcasted_iota(i32, (n, n), 1)).astype(bf16)


def gather_kernel(line, group, tab, out, lines, got):
    step = pl.program_id(0)
    width = tab.shape[0]
    per = tab.shape[1] // ROW_CHUNK
    eye = identity(128)

    def turn(c, carry):
        base = pl.multiple_of(c * ROW_CHUNK, ROW_CHUNK)
        stack = jnp.concatenate([tab[:, pl.ds(base + g * 128, 128)] for g in range(8)], axis=0)
        at = pl.multiple_of((step * per + c) * 128, 128)
        lines[pl.ds(at, 128), :] = lax.dot_general(eye, stack, NT, preferred_element_type=f32)
        return carry

    lax.fori_loop(0, per, turn, 0, unroll=8)

    @pl.when(step == pl.num_programs(0) - 1)
    def _():
        blocks, _, cap = group.shape
        batch = 4

        def serve(s, carry):
            def fetch(u, carry):
                for k in range(64):
                    j = u * 64 + k
                    got[pl.ds(j, 1), :] = lines[pl.ds(line[s * (batch * cap) + j], 1), :]
                return carry

            lax.fori_loop(0, batch * cap // 64, fetch, 0)
            turned = lax.dot_general(eye, got[...].astype(bf16), NT, preferred_element_type=f32)
            for b in range(batch):
                which = group[s * batch + b]
                rows = turned[:width, b * cap : (b + 1) * cap]
                for g in range(1, 8):
                    rows = jnp.where(which == g, turned[g * width : (g + 1) * width, b * cap : (b + 1) * cap], rows)
                out[s * batch + b] = rows.astype(bf16)
            return carry

        lax.fori_loop(0, blocks // batch, serve, 0)


def table_gather(tab_t, line, group):
    width, rows = tab_t.shape
    blocks, _, cap = group.shape
    columns = rows // 3
    return pl.pallas_call(
        gather_kernel,
        grid=(3,),
        in_specs=[smem(), vmem(), pl.BlockSpec((width, columns), lambda i: (0, i))],
        out_specs=vmem(),
        out_shape=jax.ShapeDtypeStruct((blocks, width, cap), bf16),
        scratch_shapes=[pltpu.VMEM((rows // 8, 128), f32), pltpu.VMEM((4 * cap, 128), f32)],
        compiler_params=params(),
        name="table_gather",
    )(line, group, tab_t)


def finish_kernel(n_more, line, line_v, group, returned, *refs):
    more, out, more_out = refs[:n_more], refs[n_more], refs[n_more + 1 : 2 * n_more + 1]
    lines, vals = refs[2 * n_more + 1 :]
    step = pl.program_id(0)
    per = out.shape[1] // ROW_CHUNK

    @pl.when(step == 0)
    def _():
        blocks, _, cap = group.shape

        def clear(i, carry):
            lines[pl.ds(pl.multiple_of(i * 1024, 1024), 1024), :] = jnp.zeros((1024, 128), f32)
            return carry

        lax.fori_loop(0, lines.shape[0] // 1024, clear, 0)
        batch = 32
        a = lax.div(lax.broadcasted_iota(i32, (cap, cap), 0), batch)
        near = a == lax.div(lax.broadcasted_iota(i32, (cap, cap), 1), batch)

        def serve(s, carry):
            which, own = group[s], returned[s].astype(f32)
            wide = jnp.concatenate([jnp.where(which == g, own, 0.0) for g in range(8)], axis=0)
            along = jnp.broadcast_to(line_v[s].astype(f32), (cap, cap))
            same = jnp.where(jnp.logical_and(along == along.T, near), 1.0, 0.0).astype(bf16)
            vals[...] = lax.dot_general(same, wide.astype(bf16), NT, preferred_element_type=f32)

            def add(u, carry):
                places, sums = [], []
                for k in range(batch):
                    j = u * batch + k
                    places.append(line[s * cap + j])
                    sums.append(lines[pl.ds(places[-1], 1), :] + vals[pl.ds(j, 1), :])
                for place, total in zip(places, sums):
                    lines[pl.ds(place, 1), :] = total
                return carry

            lax.fori_loop(0, cap // batch, add, 0)
            return carry

        lax.fori_loop(0, blocks, serve, 0)

    def turn(c, carry):
        width = out.shape[0]
        turned = lines[pl.ds(pl.multiple_of((step * per + c) * 128, 128), 128), :].T
        for g in range(8):
            at = pl.multiple_of(c * ROW_CHUNK + g * 128, 128)
            out[:, pl.ds(at, 128)] = turned[g * width : (g + 1) * width]
        return carry

    lax.fori_loop(0, per, turn, 0, unroll=4)
    for source, target in zip(more, more_out):
        tall, blocks, rows, lanes = source.shape
        for s in range(tall):
            for c in range(blocks):
                target[s * rows : (s + 1) * rows, c * lanes : (c + 1) * lanes] = source[s, c].astype(f32)


def finish(line, group, returned, rows, more):
    blocks, width, cap = returned.shape
    steps = 4
    in_more, out_more, shapes = [], [], []
    for x in more:
        tall, parts, r, lanes = x.shape
        if tall > 1:
            in_more.append(pl.BlockSpec((tall // steps, parts, r, lanes), lambda i: (i, 0, 0, 0)))
        else:
            in_more.append(pl.BlockSpec((1, parts, r // steps, lanes), lambda i: (0, 0, i, 0)))
        out_more.append(pl.BlockSpec((tall * r // steps, parts * lanes), lambda i: (i, 0)))
        shapes.append(jax.ShapeDtypeStruct((tall * r, parts * lanes), f32))
    return pl.pallas_call(
        functools.partial(finish_kernel, len(more)),
        grid=(steps,),
        in_specs=[smem(), vmem(), vmem(), vmem()] + in_more,
        out_specs=[pl.BlockSpec((width, rows // steps), lambda i: (0, i))] + out_more,
        out_shape=[jax.ShapeDtypeStruct((width, rows), f32)] + shapes,
        scratch_shapes=[pltpu.VMEM((rows // 8, 128), f32), pltpu.VMEM((cap, 128), f32)],
        compiler_params=params(),
        name="finish",
    )(line, line.reshape(blocks, 1, cap), group, returned, *more)


def hot(rows, index):
    column = lax.broadcasted_iota(i32, (rows, index.shape[1]), 0)
    return jnp.where(column == index, 1.0, 0.0).astype(bf16)


def count_kernel(starts, behave, counts, sums):
    owners, events, cap = counts.shape
    shift = cap.bit_length() - 1
    place = lax.broadcasted_iota(i32, (SPAN, 128), 0) * 128 + lax.broadcasted_iota(i32, (SPAN, 128), 1)
    last_block = behave.shape[0] - SPAN

    def group(e0, k):
        first, last = starts[e0], starts[e0 + GROUP]
        cuts = [starts[e0 + i] for i in range(1, GROUP)]
        b0 = lax.div(first, 128)

        def part(m):
            begin = b0 + m * SPAN
            b = jnp.minimum(begin, last_block)
            slot = behave[pl.ds(b, SPAN), :]
            p = place + b * 128
            event = jnp.zeros_like(p)
            for cut in cuts:
                event = event + jnp.where(p >= cut, 1, 0)
            key = jnp.right_shift(slot, shift) * GROUP + event
            mine = jnp.logical_and(jnp.logical_and(p >= first, p < last), p >= begin * 128)
            key = jnp.where(mine, key, -1)
            low = jnp.bitwise_and(slot, cap - 1)
            left = jnp.concatenate([hot(owners * GROUP, key[q : q + 1]) for q in range(SPAN)], axis=1)
            right = jnp.concatenate([hot(cap, low[q : q + 1]) for q in range(SPAN)], axis=1)
            return lax.dot_general(left, right, NT, preferred_element_type=f32)

        sums[k] = part(0)

        def more(m, carry):
            sums[k] += part(m)
            return carry

        lax.fori_loop(1, lax.div(last - b0 * 128 + (SPAN * 128 - 1), SPAN * 128), more, 0)

    def pair(g, carry):
        e0 = g * (2 * GROUP)
        group(e0, 0)
        group(e0 + GROUP, 1)
        for o in range(owners):
            both = [sums[k, o * GROUP : (o + 1) * GROUP, :] for k in range(2)]
            at = pl.ds(pl.multiple_of(e0, 2 * GROUP), 2 * GROUP)
            counts[o, at, :] = jnp.concatenate(both, axis=0).astype(bf16)
        return carry

    lax.fori_loop(0, events // (2 * GROUP), pair, 0)


def slot_counts(starts, behave, owners, cap):
    events = starts.shape[0] - 1
    return pl.pallas_call(
        count_kernel,
        in_specs=[smem(), vmem()],
        out_specs=vmem(),
        out_shape=jax.ShapeDtypeStruct((owners, events, cap), bf16),
        scratch_shapes=[pltpu.VMEM((2, owners * GROUP, cap), f32)],
        compiler_params=params(),
        name="slot_counts",
    )(starts, behave)


def pick_kernel(rows, live, field, counts, fields, pooled, table):
    owners, width, cap = rows.shape
    n_field, events = field.shape
    shift = cap.bit_length() - 1
    column = lax.broadcasted_iota(i32, (width, cap), 1)
    for o in range(owners):
        table[o * width : (o + 1) * width, :] = jnp.where(column < live[o], rows[o].astype(f32), 0.0).astype(bf16)

    def one(f, carry):
        slot = field[pl.ds(f, 1), :]
        owner = jnp.right_shift(slot, shift)
        got = jnp.dot(table[...], hot(cap, jnp.bitwise_and(slot, cap - 1)), preferred_element_type=f32)
        picked = got[:width]
        for o in range(1, owners):
            picked = jnp.where(owner == o, got[o * width : (o + 1) * width], picked)
        fields[pl.ds(pl.multiple_of(f * width, width), width), :] = picked.astype(bf16)
        return carry

    lax.fori_loop(0, n_field, one, 0, unroll=4)
    total = jnp.zeros((events, width), f32)
    for o in range(owners):
        total = total + lax.dot_general(counts[o], table[o * width : (o + 1) * width, :], NT, preferred_element_type=f32)
    pooled[...] = total.T


def pick_slots(rows, live, field_t, counts):
    owners, width, cap = rows.shape
    n_field, events = field_t.shape
    return pl.pallas_call(
        pick_kernel,
        in_specs=[vmem(), smem(), vmem(), vmem()],
        out_specs=[vmem(), vmem()],
        out_shape=[
            jax.ShapeDtypeStruct((n_field * width, events), bf16),
            jax.ShapeDtypeStruct((width, events), f32),
        ],
        scratch_shapes=[pltpu.VMEM((owners * width, cap), bf16)],
        compiler_params=params(),
        name="pick_slots",
    )(rows, live, field_t, counts)


def slots_back_kernel(field, d_fields, d_pooled, counts, out, total):
    owners, width, cap = out.shape
    n_field, events = field.shape
    shift = cap.bit_length() - 1
    total[...] = jnp.zeros(total.shape, f32)

    def one(f, carry):
        slot = field[pl.ds(f, 1), :]
        owner = jnp.right_shift(slot, shift)
        d = d_fields[pl.ds(pl.multiple_of(f * width, width), width), :].astype(f32)
        wide = jnp.concatenate([jnp.where(owner == o, d, 0.0).astype(bf16) for o in range(owners)], axis=0)
        total[...] += lax.dot_general(
            wide, hot(cap, jnp.bitwise_and(slot, cap - 1)), NT, preferred_element_type=f32
        )
        return carry

    lax.fori_loop(0, n_field, one, 0, unroll=2)
    for o in range(owners):
        behave = jnp.dot(d_pooled[...], counts[o], preferred_element_type=f32)
        out[o] = (total[o * width : (o + 1) * width] + behave).astype(bf16)


def slots_back(field_t, d_fields, d_pooled, counts):
    owners, _, cap = counts.shape
    width = d_pooled.shape[0]
    return pl.pallas_call(
        slots_back_kernel,
        in_specs=[vmem()] * 4,
        out_specs=vmem(),
        out_shape=jax.ShapeDtypeStruct((owners, width, cap), bf16),
        scratch_shapes=[pltpu.VMEM((owners * width, cap), f32)],
        compiler_params=params(),
        name="slots_back",
    )(field_t, d_fields, d_pooled, counts)


def place_bits():
    return [(axis, b) for axis in AXES for b in range(lax.axis_size(axis).bit_length() - 1)]


def bit_value(bit):
    return lax.rem(lax.div(lax.axis_index(bit[0]), 1 << bit[1]), 2)


def across(bit):
    axis, b = bit
    place = {a: lax.axis_index(a) for a in AXES}
    place[axis] = place[axis] + (1 - 2 * bit_value(bit)) * (1 << b)
    return tuple(place[a] for a in AXES)


class Piece:
    def __init__(self, part, inbox, total, order, sends, recvs):
        self.part, self.inbox, self.total = part, inbox, total
        self.order, self.sends, self.recvs = order, sends, recvs
        self.rows = part.shape[0]
        self.grain = self.rows >> len(order)
        self.offsets, self.copies = [0], []

    def at(self, ref, offset, n):
        return ref.at[pl.ds(pl.multiple_of(offset, self.grain), n)]

    def send(self):
        k, depth = len(self.copies), len(self.order)
        if k < depth:
            bit, half = self.order[k], self.rows >> (k + 1)
            value, offset = bit_value(bit), self.offsets[k]
            self.offsets.append(offset + value * half)
            source = self.at(self.part, offset + (1 - value) * half, half)
            target = self.inbox.at[pl.ds(self.rows - (self.rows >> k), half)]
        else:
            s = 2 * depth - 1 - k
            bit = self.order[s]
            source = target = self.at(self.total, self.offsets[s + 1], self.rows >> (s + 1))
        copy = pltpu.make_async_remote_copy(
            src_ref=source,
            dst_ref=target,
            send_sem=self.sends.at[k],
            recv_sem=self.recvs.at[k],
            device_id=across(bit),
            device_id_type=MESH,
        )
        copy.start()
        self.copies.append(copy)

    def take(self):
        k, depth = len(self.copies) - 1, len(self.order)
        self.copies[k].wait_recv()
        if k < depth:
            n, base, offset = self.rows >> (k + 1), self.rows - (self.rows >> k), self.offsets[k + 1]
            target = self.total if k == depth - 1 else self.part
            chunk = math.gcd(n, 64)

            def add(i, carry):
                at = pl.ds(pl.multiple_of(offset + i * chunk, math.gcd(self.grain, chunk)), chunk)
                came = self.inbox[pl.ds(pl.multiple_of(base + i * chunk, chunk), chunk), :]
                target[at, :] = (self.part[at, :].astype(f32) + came.astype(f32)).astype(target.dtype)
                return carry

            lax.fori_loop(0, n // chunk, add, 0)
        if k + 1 < 2 * depth:
            self.send()

    def drain(self):
        for copy in self.copies:
            copy.wait_send()


def everyone_else():
    n_wide, n_narrow = (lax.axis_size(a) for a in AXES)
    w, n = (lax.axis_index(a) for a in AXES)
    me = w * n_narrow + n
    total = n_wide * n_narrow
    for d in range(1, total):
        other = lax.rem(me + d, total)
        yield d, other, (lax.div(other, n_narrow), lax.rem(other, n_narrow))


def meet_all():
    barrier = pltpu.get_barrier_semaphore()
    for _, _, place in everyone_else():
        pl.semaphore_signal(barrier, inc=1, device_id=place, device_id_type=MESH)
    pl.semaphore_wait(barrier, lax.axis_size("wide") * lax.axis_size("narrow") - 1)


def lanes_of(rows, columns, devices):
    lanes = columns
    while lanes > 128 and (rows * (columns // lanes)) % (16 * devices):
        lanes //= 2
    return lanes


ORDERS = "BDADABGGBBBABGBAAA"


class Block:
    def __init__(self, rows, columns, devices):
        self.rows, self.columns = rows, columns
        self.lanes = lanes_of(rows, columns, devices)
        self.blocks = columns // self.lanes
        self.padded = -(-rows * self.blocks // (16 * devices)) * 16 * devices

    def put(self, piece, value):
        for c in range(self.blocks):
            piece[c * self.rows : (c + 1) * self.rows, :] = value[:, c * self.lanes : (c + 1) * self.lanes]
        extra = self.padded - self.rows * self.blocks
        if extra:
            piece[self.rows * self.blocks :, :] = jnp.zeros((extra, self.lanes), piece.dtype)

    def whole(self, total, n):
        return total[:, : self.rows * self.blocks].reshape(n, self.blocks, self.rows, self.lanes)


def orders():
    if tuple(lax.axis_size(a) for a in AXES) != (8, 4):
        return [place_bits()] * len(ORDERS)
    core, y, x, z0, z1 = ("narrow", 0), ("narrow", 1), ("wide", 0), ("wide", 1), ("wide", 2)
    ways = {
        "A": [core, x, y, z0, z1],
        "B": [core, y, x, z0, z1],
        "D": [core, z0, z1, y, x],
        "G": [core, z0, z1, x, y],
    }
    return [ways[way] for way in ORDERS]


def reduce_kernel(blocks, n_big, slot_grad, small, *refs):
    big = refs[:n_big]
    returned, small_total = refs[n_big : n_big + 2]
    totals = refs[n_big + 2 : 2 * n_big + 2]
    small_part, small_inbox = refs[2 * n_big + 2 : 2 * n_big + 4]
    parts = refs[2 * n_big + 4 : 3 * n_big + 4]
    inboxes = refs[3 * n_big + 4 : 4 * n_big + 4]
    sends, recvs, slot_sends, slot_recvs = refs[4 * n_big + 4 :]
    meet_all()
    me = lax.axis_index("wide") * lax.axis_size("narrow") + lax.axis_index("narrow")
    slot_copies = []
    for d, other, place in everyone_else():
        copy = pltpu.make_async_remote_copy(
            src_ref=slot_grad.at[other],
            dst_ref=returned.at[me],
            send_sem=slot_sends.at[d],
            recv_sem=slot_recvs.at[d],
            device_id=place,
            device_id_type=MESH,
        )
        copy.start()
        slot_copies.append(copy)
    returned[me] = slot_grad[me]
    pieces = [Piece(small_part, small_inbox, small_total, orders()[0], sends.at[0], recvs.at[0])]
    small_part[...] = small[...]
    pieces[0].send()
    for a in range(n_big):
        for i in range(parts[a].shape[0]):
            k = len(pieces)
            piece = Piece(parts[a].at[i], inboxes[a].at[i], totals[a].at[i], orders()[k - 1], sends.at[k], recvs.at[k])
            blocks[a].put(parts[a].at[i], big[a][i])
            piece.send()
            pieces.append(piece)
    for _ in range(2 * len(place_bits())):
        for piece in pieces:
            piece.take()
    for copy in slot_copies:
        copy.wait_recv()
    for copy in slot_copies:
        copy.wait_send()
    for piece in pieces:
        piece.drain()


def reduce_all(slot_grad, small, big, devices):
    blocks = [Block(x.shape[1], x.shape[2], devices) for x in big]
    shapes = [(x.shape[0], b.padded, b.lanes) for x, b in zip(big, blocks)]
    n_pieces = 1 + sum(x.shape[0] for x in big)
    steps = 2 * (devices.bit_length() - 1)
    out = pl.pallas_call(
        functools.partial(reduce_kernel, blocks, len(big)),
        in_specs=[vmem()] * (2 + len(big)),
        out_specs=[vmem()] * (2 + len(big)),
        out_shape=[jax.ShapeDtypeStruct(slot_grad.shape, bf16), jax.ShapeDtypeStruct(small.shape, f32)]
        + [jax.ShapeDtypeStruct(s, bf16) for s in shapes],
        scratch_shapes=[pltpu.VMEM(small.shape, f32)] * 2
        + [pltpu.VMEM(s, bf16) for s in shapes] * 2
        + [pltpu.SemaphoreType.DMA((n_pieces, steps))] * 2
        + [pltpu.SemaphoreType.DMA((devices,))] * 2,
        compiler_params=params(collective_id=0, has_side_effects=True),
        name="reduce_all",
    )(slot_grad, small, *big)
    return out[0], out[1], [b.whole(t, x.shape[0]) for b, t, x in zip(blocks, out[2:], big)]


def layer_norm(values, gain, shift):
    center = values - jnp.mean(values, axis=-1, keepdims=True)
    spread = jnp.mean(center * center, axis=-1, keepdims=True)
    return center * lax.rsqrt(spread + EPSILON) * gain + shift


def gelu_norm(pre, gain, shift):
    return layer_norm(jax.nn.gelu(pre), gain, shift)


def mixture(shared_logits, group_logits, outputs, onehot):
    shared_weights = jax.nn.softmax(shared_logits, axis=-1)
    shared_mix = jnp.sum(shared_weights.T[:, :, None] * outputs[:SHARED], axis=0)
    picked = jnp.sum(onehot[:, :, None] * group_logits, axis=1)
    group_weights = jax.nn.softmax(picked, axis=-1)
    domain_out = jnp.sum(onehot.T[:, :, None] * outputs[SHARED:], axis=0)
    return group_weights[:, 0:1] * shared_mix + group_weights[:, 1:2] * domain_out


def tower_head(pre_stack, tower_out, tower_out_bias, onehot):
    hidden = jax.nn.gelu(pre_stack)
    logits = jnp.sum(hidden * tower_out[:, None, :], axis=-1) + tower_out_bias[:, None]
    return jax.nn.sigmoid(jnp.sum(onehot.T * logits, axis=0))


def exact_dot(left, right):
    return jnp.dot(left, right, precision=lax.Precision.HIGHEST)


def local(
    table,
    dense,
    domains,
    lengths,
    requests,
    counts,
    field_slots,
    behave_slots,
    proj_w,
    proj_b,
    inter_gain,
    inter_bias,
    w_in,
    b_in,
    w_out,
    b_out,
    expert_gain,
    expert_bias,
    shared_gate,
    group_gate,
    tower_in,
    tower_in_bias,
    tower_out,
    tower_out_bias,
    pred_cotangent,
):
    n_wide = lax.axis_size("wide")
    n_narrow = lax.axis_size("narrow")
    devices = n_wide * n_narrow
    capacity = requests.shape[2]
    events = dense.shape[0]
    width = table.shape[1]
    sizes_seq = lengths.reshape(-1)
    starts = jnp.concatenate([jnp.zeros((1,), i32), jnp.cumsum(sizes_seq)])
    spread = slot_counts(starts, behave_slots.reshape(-1, 128), devices, capacity)
    asked = lax.all_to_all(requests, AXES, split_axis=1, concat_axis=1, tiled=True)
    asked = asked.reshape(devices, 1, capacity)
    line, group = line_of(asked), lane_group_of(asked)
    found = table_gather(table.T, line.reshape(-1), group)
    rows = lax.all_to_all(found, AXES, split_axis=0, concat_axis=0, tiled=True)
    field_t = field_slots.T
    field_width = field_t.shape[0] * width
    seq_len = sizes_seq.astype(f32)
    fields_t, pooled_sum = pick_slots(rows, counts.reshape(-1), field_t, spread)
    onehot = (domains[:, None] == jnp.arange(DOMAINS, dtype=jnp.int32)[None, :]).astype(f32)
    totals, squares, count = lax.psum(
        (exact_dot(onehot.T, dense), exact_dot(onehot.T, dense * dense), jnp.sum(onehot, axis=0)),
        ("wide", "narrow"),
    )
    count = count[:, None]
    mean = totals / count
    variance = squares / count - mean * mean
    inverse = lax.rsqrt(variance + EPSILON)
    event_inverse = exact_dot(onehot, inverse)
    centered = (dense - exact_dot(onehot, mean)) * event_inverse
    centered_low = centered.astype(bf16)
    pooled_t = (pooled_sum / seq_len[None, :]).astype(bf16)
    joined = jnp.concatenate([fields_t, pooled_t, centered_low.T], axis=0).T
    pre_proj = jnp.dot(joined, proj_w, preferred_element_type=f32) + proj_b
    state = gelu_norm(pre_proj, inter_gain, inter_bias)
    state_low = state.astype(bf16)
    kept = []
    outputs = []
    for expert in range(w_in.shape[0]):
        pre_in = jnp.dot(state_low, w_in[expert], preferred_element_type=f32) + b_in[expert]
        active = jax.nn.gelu(pre_in).astype(bf16)
        pre_out = jnp.dot(active, w_out[expert], preferred_element_type=f32) + b_out[expert]
        outputs.append(layer_norm(pre_out, expert_gain[expert], expert_bias[expert]))
        kept.append((pre_in, active, pre_out))
    outputs = jnp.stack(outputs)
    shared_logits = jnp.dot(state_low, shared_gate, preferred_element_type=f32)
    group_logits = jnp.einsum("ek,dkg->edg", state_low, group_gate, preferred_element_type=f32)

    def mixing(shared_part, group_part, expert_part):
        return mixture(shared_part, group_part, expert_part, onehot)

    mixed, mixing_back = jax.vjp(mixing, shared_logits, group_logits, outputs)
    after = state + mixed
    after_low = after.astype(bf16)
    tower_pre = (
        jnp.einsum("ek,dkj->dej", after_low, tower_in, preferred_element_type=f32)
        + tower_in_bias[:, None, :]
    )

    def heading(pre_part, out_part, bias_part):
        return tower_head(pre_part, out_part, bias_part, onehot)

    pred, heading_back = jax.vjp(heading, tower_pre, tower_out, tower_out_bias)
    d_tower_pre, d_tower_out, d_tower_out_bias = heading_back(pred_cotangent)
    d_tower_low = d_tower_pre.astype(bf16)
    d_tower_in = jnp.einsum("ek,dej->dkj", after_low, d_tower_low, preferred_element_type=f32)
    d_tower_in_bias = jnp.sum(d_tower_low.astype(f32), axis=1)
    d_after = jnp.einsum("dej,dkj->ek", d_tower_low, tower_in, preferred_element_type=f32)
    d_shared_logits, d_group_logits, d_outputs = mixing_back(d_after)
    state_wide = state_low.astype(f32)
    d_shared_gate = jnp.einsum(
        "ek,es->ks", state_wide, d_shared_logits, precision=lax.Precision.HIGHEST
    )
    d_group_gate = jnp.einsum(
        "ek,edg->dkg", state_wide, d_group_logits, precision=lax.Precision.HIGHEST
    )
    d_low = jnp.einsum(
        "es,ks->ek", d_shared_logits, shared_gate.astype(f32), precision=lax.Precision.HIGHEST
    )
    d_low = d_low + jnp.einsum(
        "edg,dkg->ek", d_group_logits, group_gate.astype(f32), precision=lax.Precision.HIGHEST
    )
    grads_w_in, grads_b_in, grads_w_out, grads_b_out, grads_gain, grads_bias = (
        [],
        [],
        [],
        [],
        [],
        [],
    )
    for expert in range(w_in.shape[0]):
        pre_in, active, pre_out = kept[expert]
        norm_back = jax.vjp(layer_norm, pre_out, expert_gain[expert], expert_bias[expert])[1]
        d_pre_out, d_gain_one, d_bias_one = norm_back(d_outputs[expert])
        d_out_low = d_pre_out.astype(bf16)
        grads_b_out.append(jnp.sum(d_out_low.astype(f32), axis=0))
        grads_w_out.append(jnp.einsum("ej,ek->jk", active, d_out_low, preferred_element_type=f32))
        d_active = jnp.einsum("ek,jk->ej", d_out_low, w_out[expert], preferred_element_type=f32)
        d_pre_in = jax.vjp(jax.nn.gelu, pre_in)[1](d_active)[0]
        d_in_low = d_pre_in.astype(bf16)
        grads_b_in.append(jnp.sum(d_in_low.astype(f32), axis=0))
        grads_w_in.append(jnp.einsum("ek,ej->kj", state_low, d_in_low, preferred_element_type=f32))
        d_low = d_low + jnp.einsum("ej,kj->ek", d_in_low, w_in[expert], preferred_element_type=f32)
        grads_gain.append(d_gain_one)
        grads_bias.append(d_bias_one)
    mixture_terms = (
        jnp.stack(grads_w_in),
        jnp.stack(grads_b_in),
        jnp.stack(grads_w_out),
        jnp.stack(grads_b_out),
        jnp.stack(grads_gain),
        jnp.stack(grads_bias),
        d_shared_gate,
        d_group_gate,
        d_tower_in,
        d_tower_in_bias,
        d_tower_out,
        d_tower_out_bias,
    )
    d_state = d_after + d_low
    d_pre_proj, d_inter_gain, d_inter_bias = jax.vjp(gelu_norm, pre_proj, inter_gain, inter_bias)[
        1
    ](d_state)
    d_proj_low = d_pre_proj.astype(bf16)
    d_proj_b = jnp.sum(d_proj_low.astype(f32), axis=0)
    d_proj_w = jnp.einsum("ef,ek->fk", joined, d_proj_low, preferred_element_type=f32)
    d_joined = jnp.einsum("ek,fk->ef", d_proj_low, proj_w, preferred_element_type=f32)
    d_centered = d_joined[:, field_width + width :]
    d_joined_t = d_joined.T
    scaled_t = d_joined_t[field_width : field_width + width] / seq_len[None, :]
    slot_grad = slots_back(field_t, d_joined_t[:field_width].astype(bf16), scaled_t.astype(bf16), spread)
    small_terms = mixture_terms[1:2] + mixture_terms[3:8] + mixture_terms[9:]
    small_terms += (d_proj_b, d_inter_gain, d_inter_bias)
    small_terms += (exact_dot(onehot.T, d_centered), exact_dot(onehot.T, d_centered * centered))
    flat = jnp.concatenate([term.reshape(-1) for term in small_terms])
    flat = jnp.pad(flat, (0, -flat.size % (devices * 1024))).reshape(-1, 128)
    n_experts, depth, units = w_in.shape
    half = units // 2
    big = (
        jnp.stack([mixture_terms[0][x, :, h * half : (h + 1) * half] for x in range(n_experts) for h in range(2)]),
        mixture_terms[2].reshape(2 * n_experts, half, depth),
        mixture_terms[8].reshape(1, -1, tower_in.shape[2]),
        d_proj_w[None],
    )
    returned, flat, totals = reduce_all(slot_grad, flat, [x.astype(bf16) for x in big], devices)
    totals[0] = totals[0].reshape(n_experts, -1, depth, totals[0].shape[3])
    d_table, d_w_in, d_w_out, d_tower_in, d_proj_w = finish(line.reshape(-1), group, returned, table.shape[0], totals)
    flat = flat.reshape(-1)
    sums, at = [], 0
    for term in small_terms:
        sums.append(flat[at : at + term.size].reshape(term.shape))
        at += term.size
    d_b_in, d_b_out, d_gain, d_bias, d_shared_gate, d_group_gate, d_tower_in_bias = sums[:7]
    d_tower_out, d_tower_out_bias, d_proj_b, d_inter_gain, d_inter_bias, sum_grad, sum_cross = sums[7:]
    d_dense = event_inverse * (
        d_centered
        - exact_dot(onehot, sum_grad / count)
        - centered * exact_dot(onehot, sum_cross / count)
    )
    return (
        pred,
        d_dense,
        d_table.T,
        d_proj_w,
        d_proj_b,
        d_inter_gain,
        d_inter_bias,
        d_w_in.reshape(w_in.shape),
        d_b_in,
        d_w_out.reshape(w_out.shape),
        d_b_out,
        d_gain,
        d_bias,
        d_shared_gate,
        d_group_gate,
        d_tower_in.reshape(tower_in.shape),
        d_tower_in_bias,
        d_tower_out,
        d_tower_out_bias,
    )


def solution(mesh):
    placed = (
        P(("wide", "narrow"), None),
        P(("wide", "narrow"), None),
        P(("wide", "narrow")),
        P(("wide", "narrow"), None),
        P(("wide", "narrow"), None, None),
        P(("wide", "narrow"), None),
        P(("wide", "narrow"), None),
        P(("wide", "narrow"), None),
        P(),
        P(),
        P(),
        P(),
        P(),
        P(),
        P(),
        P(),
        P(),
        P(),
        P(),
        P(),
        P(),
        P(),
        P(),
        P(),
        P(("wide", "narrow")),
    )
    return jax.shard_map(
        local,
        mesh=mesh,
        in_specs=placed,
        out_specs=(
            P(("wide", "narrow")),
            P(("wide", "narrow"), None),
            P(("wide", "narrow"), None),
            P(),
            P(),
            P(),
            P(),
            P(),
            P(),
            P(),
            P(),
            P(),
            P(),
            P(),
            P(),
            P(),
            P(),
            P(),
            P(),
        ),
        check_vma=False,
    )
```

profile of v0, /device:TPU:1, one launch (start us, length us, event | category | flops | bytes accessed | tf_op | source)
XLA Modules:
  0.0 407.2 jit_solution(2461318876392805449)
XLA Ops:
  0.7 1.5 copy.61
  2.1 7.1 %all-to-all-start = ((s32[1,32,256]{2,0,1:T(1,128)}), s32[1,32,256]{2,0,1:T(1,128)S(1)}, u32[]{:S(2)}, u32[]{:S(2)}) async-start(s32[1,32,256]{2,0,1:T(1,128)} %copy.61), calls=%async_computation | async-start | bytes 65536 | tf_op jit(solution)/shard_map/all_to_all | solution.py:598
  10.0 0.9 fusion.138
  10.9 0.9 fusion.124
  13.2 1.0 reduce-window.9
  14.3 0.9 fusion.195
  15.2 0.9 fusion.193
  16.1 0.9 fusion.194
  16.9 0.9 fusion.192
  17.9 39.3 %all-reduce.5 = (f32[2,16]{1,0:T(2,128)S(1)}, f32[2]{0:T(128)S(1)}, f32[2,16]{1,0:T(2,128)S(1)}) all-reduce(f32[2,16]{1,0:T(2,128)S(1)} %fusion.124, f32[2]{0:T(128)S(1)} %fusion.166, f32[2,16]{1,0:T(2,128)S(1)} %fusion.138), channel_id=1, replica_groups=mesh['wide'=8,'narrow'=4] {'wide','narrow'}, use_global_device_ids=true, to_apply=%region_5.6 | all-reduce | flops 66 | bytes 528 | tf_op jit(solution)/shard_map/psum | solution.py:608
  57.2 1.0 fusion.136
  58.9 20.9 %table_gather.1 = bf16[32,16,256]{2,1,0:T(8,128)(2,1)} custom-call(s32[8192]{0:T(1024)} %bitcast.308, s32[32,1,256]{2,1,0:T(1,128)} %get-tuple-element.146.group, bf16[16,196608]{1,0:T(8,128)(2,1)} %bitcast.301), custom_call_target="tpu_custom_call" | custom-call | tf_op jit(solution)/shard_map/table_gather/pallas_call | solution.py:101
  79.9 5.7 %all-to-all-start.1 = ((bf16[32,16,256]{2,1,0:T(8,128)(2,1)}), bf16[32,16,256]{2,1,0:T(8,128)(2,1)S(1)}, u32[]{:S(2)}, u32[]{:S(2)}) async-start(bf16[32,16,256]{2,1,0:T(8,128)(2,1)} %table_gather.1), calls=%async_computation.1 | async-start | bytes 524288 | tf_op jit(solution)/shard_map/all_to_all | solution.py:602
  86.3 28.3 %slot_counts.1.counts = bf16[32,512,256]{2,1,0:T(8,128)(2,1)} custom-call(s32[513]{0:T(1024)} %pad_add_fusion.1.starts, s32[256,128]{1,0:T(8,128)} %bitcast.314), custom_call_target="tpu_custom_call" | custom-call | tf_op jit(solution)/shard_map/slot_counts/pallas_call | solution.py:249
  115.6 14.6 %pick_slots.1 = (bf16[608,512]{1,0:T(8,128)(2,1)}, f32[16,512]{1,0:T(8,128)}) custom-call(bf16[32,16,256]{2,1,0:T(8,128)(2,1)} %copy-done.4, s32[32]{0:T(128)} %bitcast.389, s32[38,512]{1,0:T(8,128)} %bitcast.312, bf16[32,512,256]{2,1,0:T(8,128)(2,1)} %slot_counts.1.counts), custom_call_target="tpu_custom_call" | custom-call | tf_op jit(solution)/shard_map/pick_slots/pallas_call | solution.py:288
  131.0 2.0 fusion.175
  134.6 2.1 fusion.75
  139.7 1.2 fusion.197
  141.1 1.2 fusion.198
  142.5 1.2 fusion.199
  143.8 1.2 fusion.200
  147.8 0.9 multiply_reduce_fusion.11
  150.0 0.9 convert_reduce_fusion.5
  154.0 1.1 fusion.187
  155.6 1.5 fusion.67
  157.1 1.1 convert_reduce_fusion.9
  158.7 2.2 fusion.35
  161.1 2.6 convert_reduce_fusion.3
  163.7 1.1 convert_reduce_fusion.8
  164.7 2.2 fusion.36
  166.9 2.8 convert_reduce_fusion.2
  170.2 1.5 fusion.65
  171.8 1.1 convert_reduce_fusion.7
  172.8 2.2 fusion.37
  175.0 2.6 convert_reduce_fusion.1
  177.6 1.1 convert_reduce_fusion.6
  178.6 2.2 fusion.38
  180.8 2.6 convert_reduce_fusion
  184.7 1.7 fusion.31
  187.1 1.7 fusion.32
  188.8 1.1 convolution_add_fusion.2
  190.0 1.7 fusion.33
  192.4 1.7 fusion.34
  194.2 1.8 fusion.176
  195.9 1.4 multiply_reduce_fusion.2
  197.3 1.8 convert_reduce_fusion.4
  199.2 1.4 fusion.39.refs_3_
  203.1 0.9 slice.389.d_fields
  204.1 1.0 copy.77
  212.8 2.0 slice_dynamic-update-slice_fusion.7
  214.7 1.9 slice_dynamic-update-slice_fusion.6
  216.6 0.8 slice_dynamic-update-slice_fusion.5
  217.4 0.8 slice_dynamic-update-slice_fusion.4
  218.3 0.8 slice_dynamic-update-slice_fusion.3
  219.9 0.8 slice_dynamic-update-slice_fusion.1
  220.7 0.8 slice_dynamic-update-slice_fusion.refs_0_
  221.6 14.9 %slots_back.1.slot_grad = bf16[32,16,256]{2,1,0:T(8,128)(2,1)} custom-call(s32[38,512]{1,0:T(8,128)} %bitcast.313, bf16[608,512]{1,0:T(8,128)(2,1)} %slice.389.d_fields, bf16[16,512]{1,0:T(8,128)(2,1)} %fusion.121.d_pooled, bf16[32,512,256]{2,1,0:T(8,128)(2,1)} %slot_counts.1.counts), custom_call_target="tpu_custom_call" | custom-call | tf_op jit(solution)/shard_map/slots_back/pallas_call | solution.py:327
  236.5 3.6 pad_maximum_fusion
  240.1 113.5 %reduce_all.1 = (bf16[32,16,256]{2,1,0:T(8,128)(2,1)}, f32[256,128]{1,0:T(8,128)}, bf16[8,512,512]{2,1,0:T(8,128)(2,1)}, bf16[8,512,512]{2,1,0:T(8,128)(2,1)}, b...) custom-call(bf16[32,16,256]{2,1,0:T(8,128)(2,1)} %slots_back.1.slot_grad, f32[256,128]{1,0:T(8,128)} %pad_bitcast_fusion.small, ...), custom_call_target="tpu_custom_call" | custom-call | tf_op jit(solution)/shard_map/reduce_all/pallas_call | solution.py:517
  353.6 1.2 slice.286
  354.8 0.8 fusion.191
  357.1 1.4 fusion.190
  366.2 0.9 fusion.42
  367.1 39.9 %finish.1 = (f32[16,196608]{1,0:T(8,128)}, f32[2048,1024]{1,0:T(8,128)}, f32[4096,512]{1,0:T(8,128)}, f32[1024,256]{1,0:T(8,128)}, f32[640,512]{1,0:T(8,128)}) custom-call(s32[8192]{0:T(1024)} %bitcast.309, s32[32,1,256]{2,1,0:T(1,128)} %bitcast.310, s32[32,1,256]{2,1,0:T(1,128)} %get-tuple-element.146.group, ...), custom_call_target="tpu_custom_call" | custom-call | tf_op jit(solution)/shard_map/finish/pallas_call | solution.py:182
  (184 shorter events, 42.3 us)
Async XLA Ops:
  0.7 130.4 %copy-start = (bf16[640,512]{1,0:T(8,128)(2,1)S(1)}, bf16[640,512]{1,0:T(8,128)(2,1)}, u32[]{:S(2)}) copy-start(bf16[640,512]{1,0:T(8,128)(2,1)} %param.33) | copy-start | bytes 1966084
  2.1 56.1 %all-to-all-start = ((s32[1,32,256]{2,0,1:T(1,128)}), s32[1,32,256]{2,0,1:T(1,128)S(1)}, u32[]{:S(2)}, u32[]{:S(2)}) async-start(s32[1,32,256]{2,0,1:T(1,128)} %copy.61), calls=%async_computation | async-start | bytes 65536 | tf_op jit(solution)/shard_map/all_to_all | solution.py:598
  57.2 57.4 %copy-start.23 = (f32[2]{0:T(128)}, f32[2]{0:T(128)S(1)}, u32[]{:S(2)}) copy-start(f32[2]{0:T(128)S(1)} %get-tuple-element.98) | copy-start | bytes 28
  58.2 56.4 %copy-start.14 = (f32[512,16]{0,1:T(8,128)}, f32[512,16]{0,1:T(8,128)S(1)}, u32[]{:S(2)}) copy-start(f32[512,16]{0,1:T(8,128)S(1)} %fusion.136) | copy-start | bytes 98308
  58.9 27.3 %copy-start.19 = (s32[1,512]{1,0:T(1,128)S(1)}, s32[1,512]{1,0:T(1,128)}, u32[]{:S(2)}) copy-start(s32[1,512]{1,0:T(1,128)} %param.28) | copy-start | bytes 6148
  79.9 35.0 %all-to-all-start.1 = ((bf16[32,16,256]{2,1,0:T(8,128)(2,1)}), bf16[32,16,256]{2,1,0:T(8,128)(2,1)S(1)}, u32[]{:S(2)}, u32[]{:S(2)}) async-start(bf16[32,16,256]{2,1,0:T(8,128)(2,1)} %table_gather.1), calls=%async_computation.1 | async-start | bytes 524288 | tf_op jit(solution)/shard_map/all_to_all | solution.py:602
  86.2 28.3 %copy-start.12 = (s32[512]{0:T(512)S(1)}, s32[512]{0:T(512)}, u32[]{:S(2)}) copy-start(s32[512]{0:T(512)} %param.27) | copy-start | bytes 6148
  86.2 28.3 %copy-start.13 = (f32[512,16]{0,1:T(8,128)S(1)}, f32[512,16]{0,1:T(8,128)}, u32[]{:S(2)}) copy-start(f32[512,16]{0,1:T(8,128)} %param.26) | copy-start | bytes 98308
  114.9 86.2 %copy-start.10 = (f32[512,16]{0,1:T(8,128)}, f32[512,16]{0,1:T(8,128)S(1)}, u32[]{:S(2)}) copy-start(f32[512,16]{0,1:T(8,128)S(1)} %fusion.43) | copy-start | bytes 98308
  114.9 0.7 copy-start.4
  115.6 15.4 %copy-start.29 = (f32[512]{0:T(512)S(1)}, f32[512]{0:T(512)}, u32[]{:S(2)}) copy-start(f32[512]{0:T(512)} %param.34) | copy-start | bytes 6148
  131.0 2.5 copy-start.16
  131.0 2.5 copy-start.18
  133.0 1.0 copy-start.17
  133.0 1.3 copy-start.20
  134.3 2.5 copy-start.1
  137.5 2.2 copy-start.26
  139.1 4.8 %copy-start.2 = (f32[512,1024]{1,0:T(8,128)}, f32[512,1024]{1,0:T(8,128)S(1)}, u32[]{:S(2)}) copy-start(f32[512,1024]{1,0:T(8,128)S(1)} %fusion.99) | copy-start | bytes 6291460
  146.7 1.0 copy-start.9
  146.8 1.0 copy-start.21
  146.8 1.0 copy-start.30
  147.8 0.9 copy-start.25
  147.8 1.0 copy-start.22
  157.1 1.6 copy-start.3
  158.7 2.4 copy-start.27
  195.9 3.2 copy-start.28
  206.3 10.3 %copy-start.7 = (bf16[1,512,1024]{2,1,0:T(8,128)(2,1)S(1)}, bf16[1,512,1024]{2,1,0:T(8,128)(2,1)}, u32[]{:S(2)}) copy-start(bf16[1,512,1024]{2,1,0:T(8,128)(2,1)} %fusion.32) | copy-start | bytes 3145732
  212.8 5.5 %copy-start.6 = (bf16[1,512,1024]{2,1,0:T(8,128)(2,1)S(1)}, bf16[1,512,1024]{2,1,0:T(8,128)(2,1)}, u32[]{:S(2)}) copy-start(bf16[1,512,1024]{2,1,0:T(8,128)(2,1)} %fusion.33) | copy-start | bytes 3145732
  216.6 3.3 copy-start.5
  221.6 14.9 %copy-start.8 = (bf16[1,1024,512]{2,1,0:T(8,128)(2,1)S(1)}, bf16[1,1024,512]{2,1,0:T(8,128)(2,1)}, u32[]{:S(2)}) copy-start(bf16[1,1024,512]{2,1,0:T(8,128)(2,1)} %fusion.35) | copy-start | bytes 3145732
  240.1 120.0 %copy-start.24 = (f32[2]{0:T(128)S(1)}, f32[2]{0:T(128)}, u32[]{:S(2)}) copy-start(f32[2]{0:T(128)} %copy-done.23) | copy-start | bytes 28
  240.1 126.1 %copy-start.11 = (f32[512,16]{0,1:T(8,128)S(1)}, f32[512,16]{0,1:T(8,128)}, u32[]{:S(2)}) copy-start(f32[512,16]{0,1:T(8,128)} %copy-done.10) | copy-start | bytes 98308
  240.1 126.1 %copy-start.15 = (f32[512,16]{0,1:T(8,128)S(1)}, f32[512,16]{0,1:T(8,128)}, u32[]{:S(2)}) copy-start(f32[512,16]{0,1:T(8,128)} %copy-done.14) | copy-start | bytes 98308
where the time goes:
time: 413 us; the launch traced here: 407 us
  Pallas kernels  232 us (56%)
  matrix products  53.8 us (13%)
  blocking collectives  39.3 us (10%)
  local copies, waits for them, and re-layouts  35.3 us (9%)
  other arithmetic  32.3 us (8%)
  starting transfers between devices  12.8 us (3%)
    pallas_call x1, Pallas kernels, reduce_all(): pl.pallas_call(functools.partial(reduce_kernel, blocks, len(big)), in_spe...  114 us
    pallas_call x1, Pallas kernels, finish(): pl.pallas_call(functools.partial(finish_kernel, len(more)), grid=(steps,)...  39.9 us
    psum x1, blocking collectives, local(): lax.psum((exact_dot(onehot.T, dense), exact_dot(onehot.T, dense * dense),...  39.3 us
    pallas_call x1, Pallas kernels, slot_counts(): pl.pallas_call(count_kernel, in_specs=[smem(), vmem()], out_specs=vmem(),...  28.3 us
    pallas_call x1, Pallas kernels, table_gather(): pl.pallas_call(gather_kernel, grid=(3,), in_specs=[smem(), vmem(), pl.Blo...  20.9 us
    pallas_call x1, Pallas kernels, slots_back(): pl.pallas_call(slots_back_kernel, in_specs=[vmem()] * 4, out_specs=vmem()...  14.9 us
    pallas_call x1, Pallas kernels, pick_slots(): pl.pallas_call(pick_kernel, in_specs=[vmem(), smem(), vmem(), vmem()], ou...  14.6 us
    unnamed x78, local copies, waits for them, and re-layouts  14.6 us
  transfers between devices with their start and end apart: 2, of which 0 were waited for; matrix products, arithmetic and copies ran while one was open for 3% of the time, Pallas kernels for 7%

commit v1 on v0

--- a/solution.py
+++ b/solution.py
@@ -52,62 +52,6 @@
 
 def identity(n):
     return (lax.broadcasted_iota(i32, (n, n), 0) == lax.broadcasted_iota(i32, (n, n), 1)).astype(bf16)
-
-
-def gather_kernel(line, group, tab, out, lines, got):
-    step = pl.program_id(0)
-    width = tab.shape[0]
-    per = tab.shape[1] // ROW_CHUNK
-    eye = identity(128)
-
-    def turn(c, carry):
-        base = pl.multiple_of(c * ROW_CHUNK, ROW_CHUNK)
-        stack = jnp.concatenate([tab[:, pl.ds(base + g * 128, 128)] for g in range(8)], axis=0)
-        at = pl.multiple_of((step * per + c) * 128, 128)
-        lines[pl.ds(at, 128), :] = lax.dot_general(eye, stack, NT, preferred_element_type=f32)
-        return carry
-
-    lax.fori_loop(0, per, turn, 0, unroll=8)
-
-    @pl.when(step == pl.num_programs(0) - 1)
-    def _():
-        blocks, _, cap = group.shape
-        batch = 4
-
-        def serve(s, carry):
-            def fetch(u, carry):
-                for k in range(64):
-                    j = u * 64 + k
-                    got[pl.ds(j, 1), :] = lines[pl.ds(line[s * (batch * cap) + j], 1), :]
-                return carry
-
-            lax.fori_loop(0, batch * cap // 64, fetch, 0)
-            turned = lax.dot_general(eye, got[...].astype(bf16), NT, preferred_element_type=f32)
-            for b in range(batch):
-                which = group[s * batch + b]
-                rows = turned[:width, b * cap : (b + 1) * cap]
-                for g in range(1, 8):
-                    rows = jnp.where(which == g, turned[g * width : (g + 1) * width, b * cap : (b + 1) * cap], rows)
-                out[s * batch + b] = rows.astype(bf16)
-            return carry
-
-        lax.fori_loop(0, blocks // batch, serve, 0)
-
-
-def table_gather(tab_t, line, group):
-    width, rows = tab_t.shape
-    blocks, _, cap = group.shape
-    columns = rows // 3
-    return pl.pallas_call(
-        gather_kernel,
-        grid=(3,),
-        in_specs=[smem(), vmem(), pl.BlockSpec((width, columns), lambda i: (0, i))],
-        out_specs=vmem(),
-        out_shape=jax.ShapeDtypeStruct((blocks, width, cap), bf16),
-        scratch_shapes=[pltpu.VMEM((rows // 8, 128), f32), pltpu.VMEM((4 * cap, 128), f32)],
-        compiler_params=params(),
-        name="table_gather",
-    )(line, group, tab_t)
 
 
 def finish_kernel(n_more, line, line_v, group, returned, *refs):
@@ -255,48 +199,6 @@
         compiler_params=params(),
         name="slot_counts",
     )(starts, behave)
-
-
-def pick_kernel(rows, live, field, counts, fields, pooled, table):
-    owners, width, cap = rows.shape
-    n_field, events = field.shape
-    shift = cap.bit_length() - 1
-    column = lax.broadcasted_iota(i32, (width, cap), 1)
-    for o in range(owners):
-        table[o * width : (o + 1) * width, :] = jnp.where(column < live[o], rows[o].astype(f32), 0.0).astype(bf16)
-
-    def one(f, carry):
-        slot = field[pl.ds(f, 1), :]
-        owner = jnp.right_shift(slot, shift)
-        got = jnp.dot(table[...], hot(cap, jnp.bitwise_and(slot, cap - 1)), preferred_element_type=f32)
-        picked = got[:width]
-        for o in range(1, owners):
-            picked = jnp.where(owner == o, got[o * width : (o + 1) * width], picked)
-        fields[pl.ds(pl.multiple_of(f * width, width), width), :] = picked.astype(bf16)
-        return carry
-
-    lax.fori_loop(0, n_field, one, 0, unroll=4)
-    total = jnp.zeros((events, width), f32)
-    for o in range(owners):
-        total = total + lax.dot_general(counts[o], table[o * width : (o + 1) * width, :], NT, preferred_element_type=f32)
-    pooled[...] = total.T
-
-
-def pick_slots(rows, live, field_t, counts):
-    owners, width, cap = rows.shape
-    n_field, events = field_t.shape
-    return pl.pallas_call(
-        pick_kernel,
-        in_specs=[vmem(), smem(), vmem(), vmem()],
-        out_specs=[vmem(), vmem()],
-        out_shape=[
-            jax.ShapeDtypeStruct((n_field * width, events), bf16),
-            jax.ShapeDtypeStruct((width, events), f32),
-        ],
-        scratch_shapes=[pltpu.VMEM((owners * width, cap), bf16)],
-        compiler_params=params(),
-        name="pick_slots",
-    )(rows, live, field_t, counts)
 
 
 def slots_back_kernel(field, d_fields, d_pooled, counts, out, total):
@@ -530,6 +432,189 @@
     return out[0], out[1], [b.whole(t, x.shape[0]) for b, t, x in zip(blocks, out[2:], big)]
 
 
+def lookup_kernel(
+    requests, table, live, field, counts, dense, domains,
+    fields, pooled, line_out, group, stats_out,
+    tab, lines, got, line, line_smem, found, rows, slots, stats, stats_in,
+    tab_sems, line_sem, ask_sends, ask_recvs, row_sends, row_recvs, stat_sends, stat_recvs,
+):
+    owners, _, cap = requests.shape
+    width = tab.shape[0]
+    n_field, events = field.shape
+    chunks = tab_sems.shape[0]
+    part = tab.shape[1] // chunks
+    batch = 4
+    n_narrow = lax.axis_size("narrow")
+    me = lax.axis_index("wide") * n_narrow + lax.axis_index("narrow")
+
+    loads = []
+    for c in range(chunks):
+        at = pl.ds(c * part, part)
+        loads.append(pltpu.make_async_copy(table.at[:, at], tab.at[:, at], tab_sems.at[c]))
+        loads[-1].start()
+    lane = lax.broadcasted_iota(i32, (width, 128), 1)
+    mine = jnp.zeros((width, 128), f32)
+    for d in range(DOMAINS):
+        here = domains[...] == d
+        value = jnp.where(here, dense[...], 0.0)
+        one = jnp.broadcast_to(jnp.where(here, 1.0, 0.0), value.shape)
+        for k, term in enumerate((value, value * value, one)):
+            mine = jnp.where(lane == k * DOMAINS + d, jnp.sum(term, axis=1, keepdims=True), mine)
+    stats[...] = mine
+
+    meet_all()
+
+    def peer(d):
+        other = lax.rem(me + d, owners)
+        return other, (lax.div(other, n_narrow), lax.rem(other, n_narrow))
+
+    def ask(d):
+        other, place = peer(d)
+        return pltpu.make_async_remote_copy(
+            src_ref=requests.at[other], dst_ref=line.at[me], send_sem=ask_sends.at[d],
+            recv_sem=ask_recvs.at[d], device_id=place, device_id_type=MESH)
+
+    def tell(d):
+        _, place = peer(d)
+        return pltpu.make_async_remote_copy(
+            src_ref=stats, dst_ref=stats_in.at[me], send_sem=stat_sends.at[d],
+            recv_sem=stat_recvs.at[d], device_id=place, device_id_type=MESH)
+
+    def answer(d):
+        other, place = peer(d)
+        return pltpu.make_async_remote_copy(
+            src_ref=found.at[other], dst_ref=rows.at[me], send_sem=row_sends.at[d],
+            recv_sem=row_recvs.at[d], device_id=place, device_id_type=MESH)
+
+    def each(first, act):
+        def step(d, carry):
+            act(d)
+            return carry
+
+        lax.fori_loop(first, owners, step, 0)
+
+    each(1, lambda d: ask(d).start())
+    each(1, lambda d: tell(d).start())
+    line[me] = requests[me]
+    stats_in[me] = stats[...]
+
+    eye = identity(128)
+    for c in range(chunks):
+        loads[c].wait()
+
+        def turn(i, carry):
+            base = pl.multiple_of(c * part + i * ROW_CHUNK, ROW_CHUNK)
+            stack = jnp.concatenate([tab[:, pl.ds(base + g * 128, 128)] for g in range(8)], axis=0)
+            at = pl.multiple_of((c * part // ROW_CHUNK + i) * 128, 128)
+            lines[pl.ds(at, 128), :] = lax.dot_general(eye, stack, NT, preferred_element_type=f32)
+            return carry
+
+        lax.fori_loop(0, part // ROW_CHUNK, turn, 0, unroll=8)
+
+    each(1, lambda d: ask(d).wait_recv())
+    group[...] = lane_group_of(line[...])
+    line_out[...] = line_of(line[...])
+    to_smem = pltpu.make_async_copy(line_out, line_smem, line_sem)
+    to_smem.start()
+    to_smem.wait()
+
+    def serve(b, carry):
+        sources = [lax.rem(me + b * batch + k, owners) for k in range(batch)]
+        for k in range(batch):
+
+            def fetch(u, carry):
+                for i in range(64):
+                    j = u * 64 + i
+                    got[pl.ds(k * cap + j, 1), :] = lines[pl.ds(line_smem[sources[k], 0, j], 1), :]
+                return carry
+
+            lax.fori_loop(0, cap // 64, fetch, 0)
+        turned = lax.dot_general(eye, got[...].astype(bf16), NT, preferred_element_type=f32)
+        for k in range(batch):
+            which = group[sources[k]]
+            picked = turned[:width, k * cap : (k + 1) * cap]
+            for g in range(1, 8):
+                picked = jnp.where(which == g, turned[g * width : (g + 1) * width, k * cap : (k + 1) * cap], picked)
+            found[sources[k]] = picked.astype(bf16)
+        for k in range(batch):
+            d = b * batch + k
+            if k:
+                answer(d).start()
+            else:
+                pl.when(b > 0)(lambda: answer(d).start())
+        return carry
+
+    lax.fori_loop(0, owners // batch, serve, 0)
+    rows[me] = found[me]
+    each(1, lambda d: tell(d).wait_recv())
+    total = stats_in[0]
+    for o in range(1, owners):
+        total = total + stats_in[o]
+    stats_out[...] = total
+
+    each(1, lambda d: answer(d).wait_recv())
+    shift = cap.bit_length() - 1
+    column = lax.broadcasted_iota(i32, (width, cap), 1)
+    for o in range(owners):
+        slots[o * width : (o + 1) * width, :] = jnp.where(column < live[o], rows[o].astype(f32), 0.0).astype(bf16)
+
+    def one(f, carry):
+        slot = field[pl.ds(f, 1), :]
+        owner = jnp.right_shift(slot, shift)
+        all_owners = jnp.dot(slots[...], hot(cap, jnp.bitwise_and(slot, cap - 1)), preferred_element_type=f32)
+        picked = all_owners[:width]
+        for o in range(1, owners):
+            picked = jnp.where(owner == o, all_owners[o * width : (o + 1) * width], picked)
+        fields[pl.ds(pl.multiple_of(f * width, width), width), :] = picked.astype(bf16)
+        return carry
+
+    lax.fori_loop(0, n_field, one, 0, unroll=2)
+    total = jnp.zeros((events, width), f32)
+    for o in range(owners):
+        total = total + lax.dot_general(counts[o], slots[o * width : (o + 1) * width, :], NT, preferred_element_type=f32)
+    pooled[...] = total.T
+    each(1, lambda d: ask(d).wait_send())
+    each(1, lambda d: tell(d).wait_send())
+    each(1, lambda d: answer(d).wait_send())
+
+
+def lookup(requests, table_t, live, field_t, counts, dense_t, domains):
+    owners, _, cap = requests.shape
+    width, rows = table_t.shape
+    n_field, events = field_t.shape
+    chunks = 6
+    dma = pltpu.SemaphoreType.DMA
+    return pl.pallas_call(
+        lookup_kernel,
+        in_specs=[vmem(), hbm(), smem(), vmem(), vmem(), vmem(), vmem()],
+        out_specs=[vmem()] * 5,
+        out_shape=[
+            jax.ShapeDtypeStruct((n_field * width, events), bf16),
+            jax.ShapeDtypeStruct((width, events), f32),
+            jax.ShapeDtypeStruct((owners, 1, cap), i32),
+            jax.ShapeDtypeStruct((owners, 1, cap), i32),
+            jax.ShapeDtypeStruct((width, 128), f32),
+        ],
+        scratch_shapes=[
+            pltpu.VMEM((width, rows), bf16),
+            pltpu.VMEM((rows // 8, 128), f32),
+            pltpu.VMEM((4 * cap, 128), f32),
+            pltpu.VMEM((owners, 1, cap), i32),
+            pltpu.SMEM((owners, 1, cap), i32),
+            pltpu.VMEM((owners, width, cap), bf16),
+            pltpu.VMEM((owners, width, cap), bf16),
+            pltpu.VMEM((owners * width, cap), bf16),
+            pltpu.VMEM((width, 128), f32),
+            pltpu.VMEM((owners, width, 128), f32),
+            dma((chunks,)),
+            dma,
+        ]
+        + [dma((owners,))] * 6,
+        compiler_params=params(collective_id=1, has_side_effects=True),
+        name="lookup",
+    )(requests, table_t, live, field_t, counts, dense_t, domains)
+
+
 def layer_norm(values, gain, shift):
     center = values - jnp.mean(values, axis=-1, keepdims=True)
     spread = jnp.mean(center * center, axis=-1, keepdims=True)
@@ -595,21 +680,16 @@
     sizes_seq = lengths.reshape(-1)
     starts = jnp.concatenate([jnp.zeros((1,), i32), jnp.cumsum(sizes_seq)])
     spread = slot_counts(starts, behave_slots.reshape(-1, 128), devices, capacity)
-    asked = lax.all_to_all(requests, AXES, split_axis=1, concat_axis=1, tiled=True)
-    asked = asked.reshape(devices, 1, capacity)
-    line, group = line_of(asked), lane_group_of(asked)
-    found = table_gather(table.T, line.reshape(-1), group)
-    rows = lax.all_to_all(found, AXES, split_axis=0, concat_axis=0, tiled=True)
     field_t = field_slots.T
     field_width = field_t.shape[0] * width
     seq_len = sizes_seq.astype(f32)
-    fields_t, pooled_sum = pick_slots(rows, counts.reshape(-1), field_t, spread)
-    onehot = (domains[:, None] == jnp.arange(DOMAINS, dtype=jnp.int32)[None, :]).astype(f32)
-    totals, squares, count = lax.psum(
-        (exact_dot(onehot.T, dense), exact_dot(onehot.T, dense * dense), jnp.sum(onehot, axis=0)),
-        ("wide", "narrow"),
-    )
-    count = count[:, None]
+    fields_t, pooled_sum, line, group, stats = lookup(
+        requests.reshape(devices, 1, capacity), table.T, counts.reshape(-1), field_t, spread, dense.T, domains[None]
+    )
+    onehot = (domains[:, None] == jnp.arange(DOMAINS, dtype=i32)[None, :]).astype(f32)
+    totals = stats[:, :DOMAINS].T
+    squares = stats[:, DOMAINS : 2 * DOMAINS].T
+    count = stats[:1, 2 * DOMAINS : 3 * DOMAINS].T
     mean = totals / count
     variance = squares / count - mean * mean
     inverse = lax.rsqrt(variance + EPSILON)

time: 413 us -> 378 us (0.915)
  blocking collectives: 39.3 us -> 0 us
  Pallas kernels: 232 us -> 253 us
  starting transfers between devices: 12.8 us -> 0 us
  other arithmetic: 32.3 us -> 23.5 us
  local copies, waits for them, and re-layouts: 35.3 us -> 43.7 us
    psum x1 -> x0, blocking collectives: 39.3 us -> none  [local(): lax.psum((exact_dot(onehot.T, dense), exact_dot(onehot.T, dense * dense),...]
    pallas_call x2 -> x1, Pallas kernels: 35.5 us -> 57.8 us  [lookup(): pl.pallas_call(lookup_kernel, in_specs=[vmem(), hbm(), smem(), vmem(), vm...]
    all_to_all x2 -> x0, starting transfers between devices: 12.8 us -> none  [the longest x1 7.1 us: local(): lax.all_to_all(requests, AXES, split_axis=1, concat_axis=1, tiled=True)]
    unnamed x78 -> x247, local copies, waits for them, and re-layouts: 14.6 us -> 18.6 us
  transfers between devices with their start and end apart: 2 -> 0, of which waited for: 0 -> 0; matrix products, arithmetic and copies ran while one was open for 3% -> 0% of each run, Pallas kernels for 7% -> 0%
where the time goes in v1:
time: 378 us; the launch traced here: 372 us
  Pallas kernels  253 us (67%)
  matrix products  50.3 us (13%)
  local copies, waits for them, and re-layouts  43.7 us (12%)
  other arithmetic  23.5 us (6%)
    pallas_call x1, Pallas kernels, reduce_all(): pl.pallas_call(functools.partial(reduce_kernel, blocks, len(big)), in_spe...  113 us
    pallas_call x1, Pallas kernels, lookup(): pl.pallas_call(lookup_kernel, in_specs=[vmem(), hbm(), smem(), vmem(), vm...  57.8 us
    pallas_call x1, Pallas kernels, finish(): pl.pallas_call(functools.partial(finish_kernel, len(more)), grid=(steps,)...  39.9 us
    pallas_call x1, Pallas kernels, slot_counts(): pl.pallas_call(count_kernel, in_specs=[smem(), vmem()], out_specs=vmem(),...  27.3 us
    unnamed x247, local copies, waits for them, and re-layouts  18.6 us
    pallas_call x1, Pallas kernels, slots_back(): pl.pallas_call(slots_back_kernel, in_specs=[vmem()] * 4, out_specs=vmem()...  14.9 us
    dot_general x4, matrix products, local(): jnp.einsum('ek,jk->ej', d_out_low, w_out[expert], preferred_element_type=...  7.97 us

profile of v1, /device:TPU:1, one launch (start us, length us, event | category | flops | bytes accessed | tf_op | source)
XLA Modules:
  0.0 372.4 jit_solution(7949751663183271226)
XLA Ops:
  0.7 1.0 reduce-window.9
  4.8 0.9 fusion.193
  5.6 0.9 fusion.191
  6.5 0.9 fusion.192
  7.4 0.9 fusion.190
  8.3 1.4 reshape.435.requests
  9.7 27.3 %slot_counts.1.counts = bf16[32,512,256]{2,1,0:T(8,128)(2,1)} custom-call(s32[513]{0:T(1024)} %pad_add_fusion.1.starts, s32[256,128]{1,0:T(8,128)} %bitcast.312), custom_call_target="tpu_custom_call" | custom-call | tf_op jit(solution)/shard_map/slot_counts/pallas_call | solution.py:193
  37.0 57.8 %lookup.1 = (bf16[608,512]{1,0:T(8,128)(2,1)}, f32[16,512]{1,0:T(8,128)}, s32[32,1,256]{2,1,0:T(1,128)}, s32[32,1,256]{2,1,0:T(1,128)}, f32[16,128]{1,0:T(8,128)}) custom-call(s32[32,1,256]{2,1,0:T(1,128)} %reshape.435.requests, bf16[16,196608]{1,0:T(8,128)(2,1)} %bitcast.301, s32[32]{0:T(128)} %bitcast.389, s32[38,512]{1,0:T(8,128)} %bitcast.309, ...), custom_call_target="tpu_custom_call" | custom-call | tf_op jit(solution)/shard_map/lookup/pallas_call | solution.py:587
  96.4 1.0 fusion.129
  97.4 0.8 fusion.41
  99.0 2.0 fusion.173
  102.6 2.1 fusion.75
  104.8 1.2 fusion.195
  107.2 1.0 copy-done.7
  109.0 1.2 fusion.196
  112.0 1.2 fusion.197
  114.6 1.2 fusion.198
  118.2 0.9 multiply_reduce_fusion.11
  120.4 0.9 convert_reduce_fusion.5
  122.1 1.3 fusion.40
  123.4 2.0 copy.75
  126.6 3.8 %multiply_reduce_fusion.10 = (f32[512]{0:T(512)S(1)}, f32[512]{0:T(512)S(1)}, f32[512,512]{0,1:T(8,128)}, f32[512,512]{0,1:T(8,128)S(1)}, f32[512,512]{0,1:T(8,128)}) fusion(f32[512,512]{0,1:T(8,128)} %copy-done.13, f32[512,512]{0,1:T(8,128)} %copy-done.14, f32[512]{0:T(512)S(1)} %bitcast.341, f32[512]{0:T(512)S(1)} %bitcast.339, ...), kind=kOutput, calls=%fused_computation.188 | convolution fusion | flops 270007296 | bytes 6299648 | tf_op jit(solution)/shard_map/dej,dkj->ek/dot_general | solution.py:735
  130.6 1.7 broadcast_multiply_fusion.1
  132.4 1.1 convolution_bitcast_fusion.2
  133.5 1.2 fusion.167
  135.5 1.8 copy.72
  137.3 1.3 reshape.455
  138.6 1.4 convolution_bitcast_fusion
  140.1 1.3 convolution_add_fusion.4
  141.8 1.2 copy-done.15
  146.3 1.0 fusion.65
  148.2 1.0 fusion.67
  150.8 1.4 fusion.35
  153.0 2.0 convert_reduce_fusion.3
  156.7 0.8 copy-done.23
  157.6 1.2 fusion.36
  158.7 2.0 convert_reduce_fusion.2
  161.5 1.7 fusion.32
  163.2 1.2 fusion.37
  164.4 2.0 convert_reduce_fusion.1
  167.2 1.7 fusion.33
  168.9 1.6 fusion.38
  170.6 2.0 convert_reduce_fusion
  172.6 1.2 fusion.174
  173.9 2.3 pad_maximum_fusion
  176.9 1.3 convert_reduce_fusion.4
  178.2 1.4 fusion.39.refs_3_
  179.7 1.7 fusion.34
  183.8 0.9 slice.411.d_fields
  184.7 14.9 %slots_back.1.slot_grad = bf16[32,16,256]{2,1,0:T(8,128)(2,1)} custom-call(s32[38,512]{1,0:T(8,128)} %bitcast.310, bf16[608,512]{1,0:T(8,128)(2,1)} %slice.411.d_fields, bf16[16,512]{1,0:T(8,128)(2,1)} %fusion.121.d_pooled, bf16[32,512,256]{2,1,0:T(8,128)(2,1)} %slot_counts.1.counts), custom_call_target="tpu_custom_call" | custom-call | tf_op jit(solution)/shard_map/slots_back/pallas_call | solution.py:229
  199.5 0.8 slice_dynamic-update-slice_fusion.7
  200.4 0.8 slice_dynamic-update-slice_fusion.6
  201.2 0.8 slice_dynamic-update-slice_fusion.5
  202.0 0.8 slice_dynamic-update-slice_fusion.4
  202.9 0.8 slice_dynamic-update-slice_fusion.3
  203.7 0.8 slice_dynamic-update-slice_fusion.2
  204.5 0.8 slice_dynamic-update-slice_fusion.1
  205.3 0.8 slice_dynamic-update-slice_fusion.refs_0_
  206.2 112.6 %reduce_all.1 = (bf16[32,16,256]{2,1,0:T(8,128)(2,1)}, f32[256,128]{1,0:T(8,128)}, bf16[8,512,512]{2,1,0:T(8,128)(2,1)}, bf16[8,512,512]{2,1,0:T(8,128)(2,1)}, b...) custom-call(bf16[32,16,256]{2,1,0:T(8,128)(2,1)} %slots_back.1.slot_grad, f32[256,128]{1,0:T(8,128)} %pad_bitcast_fusion.small, ...), custom_call_target="tpu_custom_call" | custom-call | tf_op jit(solution)/shard_map/reduce_all/pallas_call | solution.py:419
  318.8 1.2 slice.298
  320.0 0.8 fusion.189
  321.3 0.9 fusion.43
  324.8 1.4 fusion.188
  332.3 39.9 %finish.1 = (f32[16,196608]{1,0:T(8,128)}, f32[2048,1024]{1,0:T(8,128)}, f32[4096,512]{1,0:T(8,128)}, f32[1024,256]{1,0:T(8,128)}, f32[640,512]{1,0:T(8,128)}) custom-call(s32[8192]{0:T(1024)} %bitcast.313, s32[32,1,256]{2,1,0:T(1,128)} %get-tuple-element.39.line_v, s32[32,1,256]{2,1,0:T(1,128)} %get-tuple-element.40.group, ...), custom_call_target="tpu_custom_call" | custom-call | tf_op jit(solution)/shard_map/finish/pallas_call | solution.py:126
  (345 shorter events, 40.6 us)
Async XLA Ops:
  0.7 98.3 %copy-start = (bf16[640,512]{1,0:T(8,128)(2,1)S(1)}, bf16[640,512]{1,0:T(8,128)(2,1)}, u32[]{:S(2)}) copy-start(bf16[640,512]{1,0:T(8,128)(2,1)} %param.33) | copy-start | bytes 1966084
  3.4 91.5 %copy-start.83 = (f32[1,512]{1,0:T(1,128)}, f32[1,512]{1,0:T(1,128)S(1)}, u32[]{:S(2)}) copy-start(f32[1,512]{1,0:T(1,128)S(1)} %convert_element_type.127) | copy-start | bytes 6148
  4.1 128.3 %copy-start.47 = (f32[512,2]{0,1:T(2,128)}, f32[512,2]{0,1:T(2,128)S(1)}, u32[]{:S(2)}) copy-start(f32[512,2]{0,1:T(2,128)S(1)} %fusion.143) | copy-start | bytes 12292
  4.8 105.9 %copy-start.60 = (f32[2,512]{1,0:T(2,128)}, f32[2,512]{1,0:T(2,128)S(1)}, u32[]{:S(2)}) copy-start(f32[2,512]{1,0:T(2,128)S(1)} %fusion.145) | copy-start | bytes 12292
  6.5 99.9 %copy-start.56 = (f32[1,512]{1,0:T(1,128)}, f32[1,512]{1,0:T(1,128)S(1)}, u32[]{:S(2)}) copy-start(f32[1,512]{1,0:T(1,128)S(1)} %get-tuple-element.155) | copy-start | bytes 6148
  6.5 104.0 %copy-start.54 = (f32[1,512]{1,0:T(1,128)}, f32[1,512]{1,0:T(1,128)S(1)}, u32[]{:S(2)}) copy-start(f32[1,512]{1,0:T(1,128)S(1)} %get-tuple-element.156) | copy-start | bytes 6148
  6.5 107.1 %copy-start.52 = (f32[1,512]{1,0:T(1,128)}, f32[1,512]{1,0:T(1,128)S(1)}, u32[]{:S(2)}) copy-start(f32[1,512]{1,0:T(1,128)S(1)} %get-tuple-element.154) | copy-start | bytes 6148
  6.5 109.6 %copy-start.50 = (f32[1,512]{1,0:T(1,128)}, f32[1,512]{1,0:T(1,128)S(1)}, u32[]{:S(2)}) copy-start(f32[1,512]{1,0:T(1,128)S(1)} %get-tuple-element.153) | copy-start | bytes 6148
  8.3 96.5 %copy-start.97 = (f32[1,1024]{1,0:T(1,128)}, f32[1,1024]{1,0:T(1,128)S(1)}, u32[]{:S(2)}) copy-start(f32[1,1024]{1,0:T(1,128)S(1)} %get-tuple-element.151) | copy-start | bytes 12292
  8.3 100.6 %copy-start.99 = (f32[1,1024]{1,0:T(1,128)}, f32[1,1024]{1,0:T(1,128)S(1)}, u32[]{:S(2)}) copy-start(f32[1,1024]{1,0:T(1,128)S(1)} %get-tuple-element.152) | copy-start | bytes 12292
  8.3 103.7 %copy-start.101 = (f32[1,1024]{1,0:T(1,128)}, f32[1,1024]{1,0:T(1,128)S(1)}, u32[]{:S(2)}) copy-start(f32[1,1024]{1,0:T(1,128)S(1)} %get-tuple-element.150) | copy-start | bytes 12292
  8.3 106.3 %copy-start.103 = (f32[1,1024]{1,0:T(1,128)}, f32[1,1024]{1,0:T(1,128)S(1)}, u32[]{:S(2)}) copy-start(f32[1,1024]{1,0:T(1,128)S(1)} %get-tuple-element.149) | copy-start | bytes 12292
  37.0 59.4 %copy-start.33 = (s32[512]{0:T(512)S(1)}, s32[512]{0:T(512)}, u32[]{:S(2)}) copy-start(s32[512]{0:T(512)} %param.27) | copy-start | bytes 6148
  37.0 60.4 %copy-start.34 = (f32[512,16]{0,1:T(8,128)S(1)}, f32[512,16]{0,1:T(8,128)}, u32[]{:S(2)}) copy-start(f32[512,16]{0,1:T(8,128)} %param.26) | copy-start | bytes 98308
  37.0 61.9 %copy-start.114 = (f32[512]{0:T(512)S(1)}, f32[512]{0:T(512)}, u32[]{:S(2)}) copy-start(f32[512]{0:T(512)} %param.34) | copy-start | bytes 6148
  95.7 5.3 %copy-start.89 = (bf16[16,512]{1,0:T(8,128)(2,1)}, bf16[16,512]{1,0:T(8,128)(2,1)S(1)}, u32[]{:S(2)}) copy-start(bf16[16,512]{1,0:T(8,128)(2,1)S(1)} %divide_convert_fusion) | copy-start | bytes 49156
  96.4 2.5 copy-start.106
  98.9 2.0 copy-start.91
  98.9 2.5 copy-start.63
  99.0 2.5 copy-start.93
  101.5 15.3 %copy-start.48 = (f32[512]{0:T(512)}, f32[512]{0:T(512)S(1)}, u32[]{:S(2)}) copy-start(f32[512]{0:T(512)S(1)} %fusion.153) | copy-start | bytes 6148
  102.3 2.5 copy-start.111
  102.5 29.8 %copy-start.43 = (f32[512]{0:T(512)}, f32[512]{0:T(512)S(1)}, u32[]{:S(2)}) copy-start(f32[512]{0:T(512)S(1)} %get-tuple-element.177) | copy-start | bytes 6148
  102.6 3.4 copy-start.58
  104.8 3.3 copy-start.7
  106.2 2.7 copy-start.41
  106.4 2.6 copy-start.75
  106.4 2.5 copy-start.71
  111.3 5.5 %copy-start.13 = (f32[512,512]{0,1:T(8,128)}, f32[512,512]{0,1:T(8,128)S(1)}, u32[]{:S(2)}) copy-start(f32[512,512]{0,1:T(8,128)S(1)} %fusion.28) | copy-start | bytes 3145732
  113.8 2.6 copy-start.9
  116.8 2.3 copy-start.14
  126.6 3.9 %copy-start.10 = (f32[1,512,512]{1,2,0:T(8,128)S(1)}, f32[1,512,512]{1,2,0:T(8,128)}, u32[]{:S(2)}) copy-start(f32[1,512,512]{1,2,0:T(8,128)} %copy-done.9) | copy-start | bytes 3145732
  126.6 3.9 %copy-start.12 = (f32[1,512,512]{1,2,0:T(8,128)S(1)}, f32[1,512,512]{1,2,0:T(8,128)}, u32[]{:S(2)}) copy-start(f32[1,512,512]{1,2,0:T(8,128)} %copy-done.11) | copy-start | bytes 3145732
  130.6 1.8 copy-start.62
  130.6 2.9 copy-start.59
  135.5 4.5 %copy-start.44 = (f32[512]{0:T(512)S(1)}, f32[512]{0:T(512)}, u32[]{:S(2)}) copy-start(f32[512]{0:T(512)} %copy-done.43) | copy-start | bytes 6148
  135.5 4.5 %copy-start.46 = (f32[2,512]{1,0:T(2,128)S(1)}, f32[2,512]{1,0:T(2,128)}, u32[]{:S(2)}) copy-start(f32[2,512]{1,0:T(2,128)} %copy-done.45) | copy-start | bytes 12292
  135.5 4.5 %copy-start.86 = (f32[512]{0:T(512)S(1)}, f32[512]{0:T(512)}, u32[]{:S(2)}) copy-start(f32[512]{0:T(512)} %copy-done.85) | copy-start | bytes 6148
  135.5 5.9 %copy-start.61 = (f32[2,512]{1,0:T(2,128)S(1)}, f32[2,512]{1,0:T(2,128)}, u32[]{:S(2)}) copy-start(f32[2,512]{1,0:T(2,128)} %copy-done.60) | copy-start | bytes 12292
  138.6 2.8 copy-start.17
  141.4 1.6 copy-start.15
  149.2 1.6 copy-start.25
  150.8 2.2 copy-start.112
  153.0 2.2 copy-start.8
  161.5 1.7 copy-start.21
  161.5 1.7 copy-start.100
  167.2 1.7 copy-start.19
  167.2 1.7 copy-start.98
  170.5 2.0 copy-start.29
  170.5 2.0 copy-start.64
  173.8 2.3 copy-start.49
  176.2 2.1 copy-start.90
  176.2 2.1 copy-start.92
  176.2 2.1 copy-start.113
  179.7 2.2 copy-start.32
  179.7 2.7 copy-start.88
  179.7 2.7 copy-start.94
  179.7 2.7 copy-start.95
  179.7 2.7 copy-start.108
  199.5 1.7 copy-start.26
  199.5 3.3 copy-start.27
  201.2 3.3 copy-start.28
  206.2 114.8 %copy-start.107 = (f32[2]{0:T(128)S(1)}, f32[2]{0:T(128)}, u32[]{:S(2)}) copy-start(f32[2]{0:T(128)} %copy-done.106) | copy-start | bytes 28
  206.2 115.1 %copy-start.36 = (f32[512,16]{0,1:T(8,128)S(1)}, f32[512,16]{0,1:T(8,128)}, u32[]{:S(2)}) copy-start(f32[512,16]{0,1:T(8,128)} %copy-done.35) | copy-start | bytes 98308
  (52 other events, 57.2 us)

commit v2 on v1

v2 whole, which is shorter than its diff:
```python
import functools
import math

import jax
import jax.numpy as jnp
from jax import lax
from jax.experimental import pallas as pl
from jax.experimental.pallas import tpu as pltpu
from jax.sharding import PartitionSpec as P

SHARED = 2
DOMAINS = 2

EPSILON = 1e-05

f32 = jnp.float32
bf16 = jnp.bfloat16
i32 = jnp.int32
MESH = pl.DeviceIdType.MESH
AXES = ("wide", "narrow")
NT = (((1,), (1,)), ((), ()))
TN = (((0,), (0,)), ((), ()))
VMEM_LIMIT = 60 * 1024 * 1024
ROW_CHUNK = 1024
GROUP = 8
SPAN = 6


def vmem():
    return pl.BlockSpec(memory_space=pltpu.VMEM)


def smem():
    return pl.BlockSpec(memory_space=pltpu.SMEM)


def hbm():
    return pl.BlockSpec(memory_space=pl.ANY)


def params(**more):
    return pltpu.CompilerParams(vmem_limit_bytes=VMEM_LIMIT, **more)


def line_of(rows):
    return jnp.left_shift(jnp.right_shift(rows, 10), 7) + jnp.bitwise_and(rows, 127)


def lane_group_of(rows):
    return jnp.bitwise_and(jnp.right_shift(rows, 7), 7)


def identity(n):
    return (lax.broadcasted_iota(i32, (n, n), 0) == lax.broadcasted_iota(i32, (n, n), 1)).astype(bf16)


def hot(rows, index):
    column = lax.broadcasted_iota(i32, (rows, index.shape[1]), 0)
    return jnp.where(column == index, 1.0, 0.0).astype(bf16)


def count_kernel(starts, behave, counts, sums):
    owners, events, cap = counts.shape
    shift = cap.bit_length() - 1
    place = lax.broadcasted_iota(i32, (SPAN, 128), 0) * 128 + lax.broadcasted_iota(i32, (SPAN, 128), 1)
    last_block = behave.shape[0] - SPAN

    def group(e0, k):
        first, last = starts[e0], starts[e0 + GROUP]
        cuts = [starts[e0 + i] for i in range(1, GROUP)]
        b0 = lax.div(first, 128)

        def part(m):
            begin = b0 + m * SPAN
            b = jnp.minimum(begin, last_block)
            slot = behave[pl.ds(b, SPAN), :]
            p = place + b * 128
            event = jnp.zeros_like(p)
            for cut in cuts:
                event = event + jnp.where(p >= cut, 1, 0)
            key = jnp.right_shift(slot, shift) * GROUP + event
            mine = jnp.logical_and(jnp.logical_and(p >= first, p < last), p >= begin * 128)
            key = jnp.where(mine, key, -1)
            low = jnp.bitwise_and(slot, cap - 1)
            left = jnp.concatenate([hot(owners * GROUP, key[q : q + 1]) for q in range(SPAN)], axis=1)
            right = jnp.concatenate([hot(cap, low[q : q + 1]) for q in range(SPAN)], axis=1)
            return lax.dot_general(left, right, NT, preferred_element_type=f32)

        sums[k] = part(0)

        def more(m, carry):
            sums[k] += part(m)
            return carry

        lax.fori_loop(1, lax.div(last - b0 * 128 + (SPAN * 128 - 1), SPAN * 128), more, 0)

    def pair(g, carry):
        e0 = g * (2 * GROUP)
        group(e0, 0)
        group(e0 + GROUP, 1)
        for o in range(owners):
            both = [sums[k, o * GROUP : (o + 1) * GROUP, :] for k in range(2)]
            at = pl.ds(pl.multiple_of(e0, 2 * GROUP), 2 * GROUP)
            counts[o, at, :] = jnp.concatenate(both, axis=0).astype(bf16)
        return carry

    lax.fori_loop(0, events // (2 * GROUP), pair, 0)


def slot_counts(starts, behave, owners, cap):
    events = starts.shape[0] - 1
    return pl.pallas_call(
        count_kernel,
        in_specs=[smem(), vmem()],
        out_specs=vmem(),
        out_shape=jax.ShapeDtypeStruct((owners, events, cap), bf16),
        scratch_shapes=[pltpu.VMEM((2, owners * GROUP, cap), f32)],
        compiler_params=params(),
        name="slot_counts",
    )(starts, behave)


def place_bits():
    return [(axis, b) for axis in AXES for b in range(lax.axis_size(axis).bit_length() - 1)]


def bit_value(bit):
    return lax.rem(lax.div(lax.axis_index(bit[0]), 1 << bit[1]), 2)


def across(bit):
    axis, b = bit
    place = {a: lax.axis_index(a) for a in AXES}
    place[axis] = place[axis] + (1 - 2 * bit_value(bit)) * (1 << b)
    return tuple(place[a] for a in AXES)


class Piece:
    def __init__(self, part, inbox, own, total, order, own_sem, sends, recvs):
        self.part, self.inbox, self.own, self.total = part, inbox, own, total
        self.order, self.own_sem, self.sends, self.recvs = order, own_sem, sends, recvs
        self.rows = part.shape[0]
        self.grain = self.rows >> len(order)
        self.offsets, self.copies, self.taken = [0], [], 0

    def at(self, ref, offset, n):
        return ref.at[pl.ds(pl.multiple_of(offset, self.grain), n)]

    def keep(self):
        return pltpu.make_async_copy(self.own, self.at(self.total, self.offsets[-1], self.grain), self.own_sem)

    def send(self):
        k, depth = len(self.copies), len(self.order)
        if k < depth:
            bit, half = self.order[k], self.rows >> (k + 1)
            value, offset = bit_value(bit), self.offsets[k]
            self.offsets.append(offset + value * half)
            source = self.at(self.part, offset + (1 - value) * half, half)
            target = self.inbox.at[pl.ds(self.rows - (self.rows >> k), half)]
        else:
            s = 2 * depth - 1 - k
            bit = self.order[s]
            target = self.at(self.total, self.offsets[s + 1], self.rows >> (s + 1))
            source = self.own if k == depth else target
        copy = pltpu.make_async_remote_copy(
            src_ref=source,
            dst_ref=target,
            send_sem=self.sends.at[k],
            recv_sem=self.recvs.at[k],
            device_id=across(bit),
            device_id_type=MESH,
        )
        copy.start()
        self.copies.append(copy)

    def done(self):
        return self.taken == 2 * len(self.order)

    def take(self):
        k, depth = self.taken, len(self.order)
        self.copies[k].wait_recv()
        self.taken += 1
        if k < depth:
            n, base, offset = self.rows >> (k + 1), self.rows - (self.rows >> k), self.offsets[k + 1]
            chunk = math.gcd(n, 64)

            def add(i, carry):
                at = pl.ds(pl.multiple_of(offset + i * chunk, math.gcd(self.grain, chunk)), chunk)
                came = pl.ds(pl.multiple_of(base + i * chunk, chunk), chunk)
                total = (self.part[at, :].astype(f32) + self.inbox[came, :].astype(f32)).astype(self.part.dtype)
                if k == depth - 1:
                    self.own[pl.ds(pl.multiple_of(i * chunk, chunk), chunk), :] = total
                else:
                    self.part[at, :] = total
                return carry

            lax.fori_loop(0, n // chunk, add, 0)
        if k == depth - 1:
            self.keep().start()
        if k == depth:
            self.keep().wait()
        if not self.done():
            self.send()

    def drain(self):
        for copy in self.copies:
            copy.wait_send()


def everyone_else():
    n_wide, n_narrow = (lax.axis_size(a) for a in AXES)
    w, n = (lax.axis_index(a) for a in AXES)
    me = w * n_narrow + n
    total = n_wide * n_narrow
    for d in range(1, total):
        other = lax.rem(me + d, total)
        yield d, other, (lax.div(other, n_narrow), lax.rem(other, n_narrow))


def greet_all():
    barrier = pltpu.get_barrier_semaphore()
    for _, _, place in everyone_else():
        pl.semaphore_signal(barrier, inc=1, device_id=place, device_id_type=MESH)


def wait_for_all():
    pl.semaphore_wait(pltpu.get_barrier_semaphore(), lax.axis_size("wide") * lax.axis_size("narrow") - 1)


def meet_all():
    greet_all()
    wait_for_all()


def lanes_of(rows, columns, devices):
    lanes = columns
    while lanes > 128 and (rows * (columns // lanes)) % (16 * devices):
        lanes //= 2
    return lanes


ORDERS = "BDADABGGBBBABGBAAA"


class Block:
    def __init__(self, rows, columns, devices):
        self.rows, self.columns = rows, columns
        self.lanes = lanes_of(rows, columns, devices)
        self.blocks = columns // self.lanes
        self.padded = -(-rows * self.blocks // (16 * devices)) * 16 * devices

    def put(self, piece, value):
        for c in range(self.blocks):
            piece[c * self.rows : (c + 1) * self.rows, :] = value[:, c * self.lanes : (c + 1) * self.lanes]
        extra = self.padded - self.rows * self.blocks
        if extra:
            piece[self.rows * self.blocks :, :] = jnp.zeros((extra, self.lanes), piece.dtype)

    def whole(self, total, n):
        return total[:, : self.rows * self.blocks].reshape(n, self.blocks, self.rows, self.lanes)


def orders():
    if tuple(lax.axis_size(a) for a in AXES) != (8, 4):
        return [place_bits()] * len(ORDERS)
    core, y, x, z0, z1 = ("narrow", 0), ("narrow", 1), ("wide", 0), ("wide", 1), ("wide", 2)
    ways = {
        "A": [core, x, y, z0, z1],
        "B": [core, y, x, z0, z1],
        "D": [core, z0, z1, y, x],
        "G": [core, z0, z1, x, y],
    }
    return [ways[way] for way in ORDERS]


def lookup_kernel(
    requests, table, live, field, counts, dense, domains,
    fields, pooled, line_out, group, stats_out,
    tab, lines, got, line, line_smem, found, rows, slots, stats, stats_in,
    tab_sems, line_sem, ask_sends, ask_recvs, row_sends, row_recvs, stat_sends, stat_recvs,
):
    owners, _, cap = requests.shape
    width = tab.shape[0]
    n_field, events = field.shape
    chunks = tab_sems.shape[0]
    part = tab.shape[1] // chunks
    batch = 4
    n_narrow = lax.axis_size("narrow")
    me = lax.axis_index("wide") * n_narrow + lax.axis_index("narrow")

    loads = []
    for c in range(chunks):
        at = pl.ds(c * part, part)
        loads.append(pltpu.make_async_copy(table.at[:, at], tab.at[:, at], tab_sems.at[c]))
        loads[-1].start()
    lane = lax.broadcasted_iota(i32, (width, 128), 1)
    mine = jnp.zeros((width, 128), f32)
    for d in range(DOMAINS):
        here = domains[...] == d
        value = jnp.where(here, dense[...], 0.0)
        one = jnp.broadcast_to(jnp.where(here, 1.0, 0.0), value.shape)
        for k, term in enumerate((value, value * value, one)):
            mine = jnp.where(lane == k * DOMAINS + d, jnp.sum(term, axis=1, keepdims=True), mine)
    stats[...] = mine

    meet_all()

    def peer(d):
        other = lax.rem(me + d, owners)
        return other, (lax.div(other, n_narrow), lax.rem(other, n_narrow))

    def ask(d):
        other, place = peer(d)
        return pltpu.make_async_remote_copy(
            src_ref=requests.at[other], dst_ref=line.at[me], send_sem=ask_sends.at[d],
            recv_sem=ask_recvs.at[d], device_id=place, device_id_type=MESH)

    def tell(d):
        _, place = peer(d)
        return pltpu.make_async_remote_copy(
            src_ref=stats, dst_ref=stats_in.at[me], send_sem=stat_sends.at[d],
            recv_sem=stat_recvs.at[d], device_id=place, device_id_type=MESH)

    def answer(d):
        other, place = peer(d)
        return pltpu.make_async_remote_copy(
            src_ref=found.at[other], dst_ref=rows.at[me], send_sem=row_sends.at[d],
            recv_sem=row_recvs.at[d], device_id=place, device_id_type=MESH)

    def each(first, act):
        def step(d, carry):
            act(d)
            return carry

        lax.fori_loop(first, owners, step, 0)

    each(1, lambda d: ask(d).start())
    each(1, lambda d: tell(d).start())
    line[me] = requests[me]
    stats_in[me] = stats[...]

    eye = identity(128)
    for c in range(chunks):
        loads[c].wait()

        def turn(i, carry):
            base = pl.multiple_of(c * part + i * ROW_CHUNK, ROW_CHUNK)
            stack = jnp.concatenate([tab[:, pl.ds(base + g * 128, 128)] for g in range(8)], axis=0)
            at = pl.multiple_of((c * part // ROW_CHUNK + i) * 128, 128)
            lines[pl.ds(at, 128), :] = lax.dot_general(eye, stack, NT, preferred_element_type=f32)
            return carry

        lax.fori_loop(0, part // ROW_CHUNK, turn, 0, unroll=8)

    each(1, lambda d: ask(d).wait_recv())
    group[...] = lane_group_of(line[...])
    line_out[...] = line_of(line[...])
    to_smem = pltpu.make_async_copy(line_out, line_smem, line_sem)
    to_smem.start()
    to_smem.wait()

    def serve(b, carry):
        sources = [lax.rem(me + b * batch + k, owners) for k in range(batch)]
        for k in range(batch):

            def fetch(u, carry):
                for i in range(64):
                    j = u * 64 + i
                    got[pl.ds(k * cap + j, 1), :] = lines[pl.ds(line_smem[sources[k], 0, j], 1), :]
                return carry

            lax.fori_loop(0, cap // 64, fetch, 0)
        turned = lax.dot_general(eye, got[...].astype(bf16), NT, preferred_element_type=f32)
        for k in range(batch):
            which = group[sources[k]]
            picked = turned[:width, k * cap : (k + 1) * cap]
            for g in range(1, 8):
                picked = jnp.where(which == g, turned[g * width : (g + 1) * width, k * cap : (k + 1) * cap], picked)
            found[sources[k]] = picked.astype(bf16)
        for k in range(batch):
            d = b * batch + k
            if k:
                answer(d).start()
            else:
                pl.when(b > 0)(lambda: answer(d).start())
        return carry

    lax.fori_loop(0, owners // batch, serve, 0)
    rows[me] = found[me]
    each(1, lambda d: tell(d).wait_recv())
    total = stats_in[0]
    for o in range(1, owners):
        total = total + stats_in[o]
    stats_out[...] = total

    each(1, lambda d: answer(d).wait_recv())
    shift = cap.bit_length() - 1
    column = lax.broadcasted_iota(i32, (width, cap), 1)
    for o in range(owners):
        slots[o * width : (o + 1) * width, :] = jnp.where(column < live[o], rows[o].astype(f32), 0.0).astype(bf16)

    def one(f, carry):
        slot = field[pl.ds(f, 1), :]
        owner = jnp.right_shift(slot, shift)
        all_owners = jnp.dot(slots[...], hot(cap, jnp.bitwise_and(slot, cap - 1)), preferred_element_type=f32)
        picked = all_owners[:width]
        for o in range(1, owners):
            picked = jnp.where(owner == o, all_owners[o * width : (o + 1) * width], picked)
        fields[pl.ds(pl.multiple_of(f * width, width), width), :] = picked.astype(bf16)
        return carry

    lax.fori_loop(0, n_field, one, 0, unroll=2)
    total = jnp.zeros((events, width), f32)
    for o in range(owners):
        total = total + lax.dot_general(counts[o], slots[o * width : (o + 1) * width, :], NT, preferred_element_type=f32)
    pooled[...] = total.T
    each(1, lambda d: ask(d).wait_send())
    each(1, lambda d: tell(d).wait_send())
    each(1, lambda d: answer(d).wait_send())


def lookup(requests, table_t, live, field_t, counts, dense_t, domains):
    owners, _, cap = requests.shape
    width, rows = table_t.shape
    n_field, events = field_t.shape
    chunks = 6
    dma = pltpu.SemaphoreType.DMA
    return pl.pallas_call(
        lookup_kernel,
        in_specs=[vmem(), hbm(), smem(), vmem(), vmem(), vmem(), vmem()],
        out_specs=[vmem()] * 5,
        out_shape=[
            jax.ShapeDtypeStruct((n_field * width, events), bf16),
            jax.ShapeDtypeStruct((width, events), f32),
            jax.ShapeDtypeStruct((owners, 1, cap), i32),
            jax.ShapeDtypeStruct((owners, 1, cap), i32),
            jax.ShapeDtypeStruct((width, 128), f32),
        ],
        scratch_shapes=[
            pltpu.VMEM((width, rows), bf16),
            pltpu.VMEM((rows // 8, 128), f32),
            pltpu.VMEM((4 * cap, 128), f32),
            pltpu.VMEM((owners, 1, cap), i32),
            pltpu.SMEM((owners, 1, cap), i32),
            pltpu.VMEM((owners, width, cap), bf16),
            pltpu.VMEM((owners, width, cap), bf16),
            pltpu.VMEM((owners * width, cap), bf16),
            pltpu.VMEM((width, 128), f32),
            pltpu.VMEM((owners, width, 128), f32),
            dma((chunks,)),
            dma,
        ]
        + [dma((owners,))] * 6,
        compiler_params=params(collective_id=1, has_side_effects=True),
        name="lookup",
    )(requests, table_t, live, field_t, counts, dense_t, domains)


STRIPE = 64
GATE_ROWS = 16
GELU_SCALE = math.sqrt(2.0 / math.pi)
GELU_CUBE = 0.044715


def gelu_and_slope(x):
    square = x * x
    t = jnp.tanh(GELU_SCALE * (x + GELU_CUBE * (square * x)))
    half = 0.5 * (1.0 + t)
    return x * half, half + 0.5 * x * (1.0 - t * t) * (GELU_SCALE * (1.0 + 3.0 * GELU_CUBE * square))


def standardise(values):
    center = values - jnp.mean(values, axis=-1, keepdims=True)
    inverse = lax.rsqrt(jnp.mean(center * center, axis=-1, keepdims=True) + EPSILON)
    return center * inverse, inverse


def standardise_back(d, standard, inverse):
    along = jnp.mean(d * standard, axis=-1, keepdims=True)
    return inverse * (d - jnp.mean(d, axis=-1, keepdims=True) - standard * along)


def loop(n, body):
    def step(i, carry):
        body(i)
        return carry

    lax.fori_loop(0, n, step, 0)


def columns(rows):
    have = rows.shape[0]
    if have < 8:
        rows = jnp.concatenate([rows, jnp.zeros((8 - have, rows.shape[1]), f32)], axis=0)
    return rows.T


def thirds(x):
    high = x.astype(bf16)
    rest = x - high.astype(f32)
    middle = rest.astype(bf16)
    return jnp.concatenate([high, middle, (rest - middle.astype(f32)).astype(bf16)], axis=0)


def domain_moments(stats):
    result = []
    for d in range(DOMAINS):
        count = stats[:, 2 * DOMAINS + d : 2 * DOMAINS + d + 1]
        mean = stats[:, d : d + 1] / count
        variance = stats[:, DOMAINS + d : DOMAINS + d + 1] / count - mean * mean
        result.append((mean, lax.rsqrt(variance + EPSILON), count))
    return result


def by_domain(domains, values):
    picked = values[0]
    for d in range(1, DOMAINS):
        picked = jnp.where(domains == d, values[d], picked)
    return picked


class Rows:
    def __init__(self, experts, units, depth, tower, width):
        self.next = 0
        lines = lambda n: -(-n // 128)
        self.b_in = [self.take(lines(units)) for _ in range(experts)]
        self.b_out, self.gain, self.bias = ([self.take(lines(depth)) for _ in range(experts)] for _ in range(3))
        self.proj_b, self.inter_gain, self.inter_bias = (self.take(lines(depth)) for _ in range(3))
        self.gates = [self.take(lines(depth)) for _ in range(SHARED + 2 * DOMAINS)]
        self.tower_in_bias, self.tower_out = ([self.take(lines(tower)) for _ in range(DOMAINS)] for _ in range(2))
        self.tower_out_bias = self.take(1)
        self.dense = self.take(width)

    def take(self, n):
        at, self.next = self.next, self.next + n
        return at

    def padded(self, devices):
        return -(-self.next // (8 * devices)) * 8 * devices


def put_row(small, at, row):
    for c in range(row.shape[1] // 128):
        small[at + c : at + c + 1, :] = row[:, c * 128 : (c + 1) * 128]


def learn_kernel(
    shape, blocks,
    fields, pooled, lengths, dense, domains, cotangent, stats, proj_w, proj_b, inter_gain, inter_bias,
    w_in_hbm, b_in, w_out_hbm, b_out, expert_gain, expert_bias, gates, tower_in, tower_in_bias, tower_out,
    tower_out_bias, field, counts_hbm,
    pred, centered, d_centered, returned, small_total, total_in, total_out, total_tower, total_proj,
    w_in, w_out, joined, joined_rows, pre_slope, pre_standard, pre_inverse, state_low, state_turned, coef,
    active, slope, standard, inverse, work, after, after_low, after_turned, d_tower, d_after, d_state, products,
    d_out, d_in, d_fields, d_pooled, counts, slot_total, slot_grad,
    small_part, small_inbox, part_in, part_out, part_tower, part_proj, inbox_in, inbox_out, inbox_tower, inbox_proj,
    small_own, own_in, own_out, own_tower, own_proj, in_sems, out_sems, count_sems, own_sems, sends, recvs, slot_sends, slot_recvs,
):
    experts, depth, units = w_in.shape
    width, events = dense.shape
    n_field = field.shape[0]
    owners, _, cap = slot_grad.shape
    tower_units = tower_in.shape[2]
    greet_all()
    for x in range(experts):
        pltpu.make_async_copy(w_in_hbm.at[x], w_in.at[x], in_sems.at[x]).start()
        pltpu.make_async_copy(w_out_hbm.at[x], w_out.at[x], out_sems.at[x]).start()

    which = domains[...]
    moments = domain_moments(stats[...])
    mean, scale = (by_domain(which, [m[i] for m in moments]) for i in range(2))
    centered[...] = (dense[...] - mean) * scale
    joined[: n_field * width, :] = fields[...]
    joined[n_field * width : (n_field + 1) * width, :] = (pooled[...] / lengths[...]).astype(bf16)
    joined[(n_field + 1) * width :, :] = centered[...].astype(bf16)
    joined_rows[...] = joined[...].T
    quarter = 256

    def project(c):
        at = pl.ds(pl.multiple_of(c * quarter, quarter), quarter)
        work[:, at] = jnp.dot(joined_rows[...], proj_w[:, at], preferred_element_type=f32) + proj_b[:, at]

    loop(depth // quarter, project)

    def stripe(i):
        return pl.ds(pl.multiple_of(i * STRIPE, STRIPE), STRIPE)

    def start_state(i):
        at = stripe(i)
        value, pre_slope[at, :] = gelu_and_slope(work[at, :])
        pre_standard[at, :], pre_inverse[at, :] = standardise(value)
        state = pre_standard[at, :] * inter_gain[...] + inter_bias[...]
        after[at, :] = state
        state_low[at, :] = state.astype(bf16)

    loop(events // STRIPE, start_state)
    state_turned[...] = state_low[...].T
    logits = lax.dot_general(gates[...], state_low[...], NT, preferred_element_type=f32)

    def softmax_pair(a, b):
        top = jnp.maximum(a, b)
        a, b = jnp.exp(a - top), jnp.exp(b - top)
        return a / (a + b), b / (a + b)

    share = softmax_pair(logits[0:1], logits[1:2])
    group_logits = [
        by_domain(which, [logits[SHARED + 2 * d + i : SHARED + 2 * d + i + 1] for d in range(DOMAINS)]) for i in range(2)
    ]
    level = softmax_pair(*group_logits)
    here = [jnp.where(which == d, 1.0, 0.0) for d in range(DOMAINS)]
    weights = [level[0] * share[0], level[0] * share[1]] + [level[1] * here[d] for d in range(DOMAINS)]
    weight_columns = columns(jnp.concatenate(weights, axis=0))
    coef[...] = weight_columns

    def expert_forward(x):
        pltpu.make_async_copy(w_in_hbm.at[x], w_in.at[x], in_sems.at[x]).wait()

        def enter(c):
            at = pl.ds(pl.multiple_of(c * quarter, quarter), quarter)
            pre = jnp.dot(state_low[...], w_in[x, :, at], preferred_element_type=f32) + b_in[x, :, at]
            value, rise = gelu_and_slope(pre)
            active[x, :, at] = value.astype(bf16)
            slope[x, :, at] = rise.astype(bf16)

        loop(units // quarter, enter)
        pltpu.make_async_copy(w_out_hbm.at[x], w_out.at[x], out_sems.at[x]).wait()

        def leave(c):
            at = pl.ds(pl.multiple_of(c * quarter, quarter), quarter)
            work[:, at] = jnp.dot(active[x], w_out[x, :, at], preferred_element_type=f32) + b_out[x, :, at]

        loop(depth // quarter, leave)

        def mix(i):
            at = stripe(i)
            value, inverse[at, x : x + 1] = standardise(work[at, :])
            standard[x, at, :] = value.astype(bf16)
            after[at, :] += coef[at, x : x + 1] * (value * expert_gain[x] + expert_bias[x])

        loop(events // STRIPE, mix)

    for x in range(experts):
        expert_forward(x)
    after_low[...] = after[...].astype(bf16)
    after_turned[...] = after_low[...].T

    here_columns = columns(jnp.concatenate(here + [cotangent[...]], axis=0))
    logit = jnp.zeros((events, 1), f32)
    for d in range(DOMAINS):
        pre = jnp.dot(after_low[...], tower_in[d], preferred_element_type=f32) + tower_in_bias[d : d + 1, :]
        value, rise = gelu_and_slope(pre)
        work[:, d * tower_units : (d + 1) * tower_units] = value
        d_after[:, d * tower_units : (d + 1) * tower_units] = rise
        head = jnp.sum(value * tower_out[d : d + 1, :], axis=1, keepdims=True) + tower_out_bias[:, d : d + 1]
        logit = logit + here_columns[:, d : d + 1] * head
    chance = 1.0 / (1.0 + jnp.exp(-logit))
    d_logit = here_columns[:, DOMAINS : DOMAINS + 1] * chance * (1.0 - chance)
    pred[...] = jnp.broadcast_to(chance, (events, 8)).T[0:1, :]
    lane = lax.broadcasted_iota(i32, (1, 128), 1)
    bias_row = jnp.zeros((1, 128), f32)
    for d in range(DOMAINS):
        at = slice(d * tower_units, (d + 1) * tower_units)
        mine = d_logit * here_columns[:, d : d + 1]
        put_row(small_part, shape.tower_out[d], jnp.sum(mine * work[:, at], axis=0, keepdims=True))
        bias_row = jnp.where(lane == d, jnp.sum(mine, axis=0, keepdims=True), bias_row)
        low = (mine * tower_out[d : d + 1, :] * d_after[:, at]).astype(bf16)
        d_tower[d] = low
        put_row(small_part, shape.tower_in_bias[d], jnp.sum(low.astype(f32), axis=0, keepdims=True))
    small_part[shape.tower_out_bias : shape.tower_out_bias + 1, :] = bias_row

    wait_for_all()
    ways = orders()
    pieces = []

    def send(block, parts, inboxes, owns, totals, i, value):
        k = len(pieces)
        block.put(parts.at[i], value)
        piece = Piece(
            parts.at[i], inboxes.at[i], owns.at[i], totals.at[i], ways[k], own_sems.at[k], sends.at[k], recvs.at[k]
        )
        piece.send()
        pieces.append(piece)

    towers = [jnp.dot(after_turned[...], d_tower[d], preferred_element_type=f32).astype(bf16) for d in range(DOMAINS)]
    send(blocks[2], part_tower, inbox_tower, own_tower, total_tower, 0, jnp.concatenate(towers, axis=0))
    d_after[...] = sum(
        lax.dot_general(d_tower[d], tower_in[d], NT, preferred_element_type=f32) for d in range(DOMAINS)
    )
    d_state[...] = d_after[...]

    products[...] = jnp.zeros(products.shape, f32)
    zero = jnp.zeros((1, depth), f32)
    half = units // 2
    for x in range(experts):

        def unmix(i, sums):
            at = stripe(i)
            d, value = d_after[at, :], standard[x, at, :].astype(f32)
            products[at, x : x + 1] = jnp.sum(d * (value * expert_gain[x] + expert_bias[x]), axis=1, keepdims=True)
            d = coef[at, x : x + 1] * d
            low = standardise_back(d * expert_gain[x], value, inverse[at, x : x + 1]).astype(bf16)
            d_out[at, :] = low
            terms = (d * value, d, low.astype(f32))
            return tuple(s + jnp.sum(t, axis=0, keepdims=True) for s, t in zip(sums, terms))

        for place, row in zip((shape.gain[x], shape.bias[x], shape.b_out[x]),
                              lax.fori_loop(0, events // STRIPE, unmix, (zero,) * 3)):
            put_row(small_part, place, row)
        older = list(pieces)
        for h in range(2):
            value = lax.dot_general(active[x, :, h * half : (h + 1) * half], d_out[...], TN, preferred_element_type=f32)
            send(blocks[1], part_out, inbox_out, own_out, total_out, 2 * x + h, value.astype(bf16))

        def unenter(c):
            at = pl.ds(pl.multiple_of(c * quarter, quarter), quarter)
            d = lax.dot_general(d_out[...], w_out[x, at, :], NT, preferred_element_type=f32)
            low = (d * slope[x, :, at].astype(f32)).astype(bf16)
            d_in[:, at] = low
            row = jnp.sum(low.astype(f32), axis=0, keepdims=True)
            for q in range(quarter // 128):
                small_part[pl.ds(shape.b_in[x] + c * (quarter // 128) + q, 1), :] = row[:, q * 128 : (q + 1) * 128]

        loop(units // quarter, unenter)
        for h in range(2):
            value = jnp.dot(state_turned[...], d_in[:, h * half : (h + 1) * half], preferred_element_type=f32)
            send(blocks[0], part_in, inbox_in, own_in, total_in, 2 * x + h, value.astype(bf16))

        def unstate(c):
            at = pl.ds(pl.multiple_of(c * quarter, quarter), quarter)
            d_state[:, at] += lax.dot_general(d_in[...], w_in[x, at, :], NT, preferred_element_type=f32)

        loop(depth // quarter, unstate)
        for piece in older:
            piece.take()

    q = products[...].T
    q = [q[x : x + 1] for x in range(experts)]
    d_level = (share[0] * q[0] + share[1] * q[1], by_domain(which, q[SHARED:]))
    mean_share = share[0] * q[0] + share[1] * q[1]
    d_share = [level[0] * share[s] * (q[s] - mean_share) for s in range(SHARED)]
    mean_level = level[0] * d_level[0] + level[1] * d_level[1]
    d_group = [level[i] * (d_level[i] - mean_level) for i in range(2)]
    rows = d_share + [d_group[i] * here[d] for d in range(DOMAINS) for i in range(2)]
    d_logits = jnp.concatenate(rows + [jnp.zeros((GATE_ROWS - len(rows), events), f32)], axis=0)
    split = thirds(d_logits)
    gate_sums = jnp.dot(split, state_low[...], preferred_element_type=f32)
    gate_sums = sum(gate_sums[i * GATE_ROWS : (i + 1) * GATE_ROWS] for i in range(3))
    for i, place in enumerate(shape.gates):
        put_row(small_part, place, gate_sums[i : i + 1])
    gates_thrice = jnp.concatenate([gates[...]] * 3, axis=0)
    d_state[...] += lax.dot_general(split, gates_thrice, TN, preferred_element_type=f32)

    def unstart(i, sums):
        at = stripe(i)
        d, value = d_state[at, :], pre_standard[at, :]
        low = (standardise_back(d * inter_gain[...], value, pre_inverse[at, :]) * pre_slope[at, :]).astype(bf16)
        d_out[at, :] = low
        terms = (d * value, d, low.astype(f32))
        return tuple(s + jnp.sum(t, axis=0, keepdims=True) for s, t in zip(sums, terms))

    for place, row in zip((shape.inter_gain, shape.inter_bias, shape.proj_b),
                          lax.fori_loop(0, events // STRIPE, unstart, (zero,) * 3)):
        put_row(small_part, place, row)
    value = jnp.dot(joined[...], d_out[...], preferred_element_type=f32)
    send(blocks[3], part_proj, inbox_proj, own_proj, total_proj, 0, value.astype(bf16))
    ahead = counts.shape[0]

    def fetch(o):
        slot = o % ahead if isinstance(o, int) else lax.rem(o, ahead)
        return pltpu.make_async_copy(counts_hbm.at[o], counts.at[slot], count_sems.at[slot])

    for o in range(ahead):
        fetch(o).start()
    n_all = n_field * width
    d_fields[...] = lax.dot_general(proj_w[:n_all, :], d_out[...], NT, preferred_element_type=f32).astype(bf16)
    tail = lax.dot_general(proj_w[n_all:, :], d_out[...], NT, preferred_element_type=f32)
    d_pooled[...] = (tail[:width] / lengths[...]).astype(bf16)
    d_centered[...] = tail[width:]
    lanes = lax.broadcasted_iota(i32, (width, 128), 1)
    sums = jnp.zeros((width, 128), f32)
    for d in range(DOMAINS):
        mine = jnp.where(which == d, tail[width:], 0.0)
        for k, term in enumerate((mine, mine * centered[...])):
            sums = jnp.where(lanes == k * DOMAINS + d, jnp.sum(term, axis=1, keepdims=True), sums)
    small_part[shape.dense : shape.dense + width, :] = sums
    if small_part.shape[0] > shape.next:
        small_part[shape.next :, :] = jnp.zeros((small_part.shape[0] - shape.next, 128), f32)
    k = len(pieces)
    small_piece = Piece(
        small_part, small_inbox, small_own, small_total, ways[0], own_sems.at[k], sends.at[k], recvs.at[k]
    )
    small_piece.send()
    for piece in pieces:
        piece.take()
    pieces.append(small_piece)

    shift = cap.bit_length() - 1
    slot_total[...] = jnp.zeros(slot_total.shape, f32)

    def scatter(f, carry):
        slot = field[pl.ds(f, 1), :]
        owner = jnp.right_shift(slot, shift)
        d = d_fields[pl.ds(pl.multiple_of(f * width, width), width), :].astype(f32)
        wide = jnp.concatenate([jnp.where(owner == o, d, 0.0).astype(bf16) for o in range(owners)], axis=0)
        slot_total[...] += lax.dot_general(
            wide, hot(cap, jnp.bitwise_and(slot, cap - 1)), NT, preferred_element_type=f32
        )
        return carry

    def scatter_some(first, last):
        lax.fori_loop(first, last, scatter, 0)

    middle = n_field // 2
    scatter_some(0, middle)
    for piece in pieces:
        piece.take()
    scatter_some(middle, n_field)

    def spread(o):
        fetch(o).wait()
        behave = jnp.dot(d_pooled[...], counts[lax.rem(o, ahead)], preferred_element_type=f32)
        at = pl.ds(pl.multiple_of(o * width, width), width)
        slot_grad[o] = (slot_total[at, :] + behave).astype(bf16)
        pl.when(o + ahead < owners)(lambda: fetch(o + ahead).start())

    loop(owners, spread)
    me = lax.axis_index("wide") * lax.axis_size("narrow") + lax.axis_index("narrow")
    slot_copies = []
    for d, other, place in everyone_else():
        copy = pltpu.make_async_remote_copy(
            src_ref=slot_grad.at[other], dst_ref=returned.at[me], send_sem=slot_sends.at[d],
            recv_sem=slot_recvs.at[d], device_id=place, device_id_type=MESH)
        copy.start()
        slot_copies.append(copy)
    returned[me] = slot_grad[me]

    while any(not piece.done() for piece in pieces):
        for piece in pieces:
            if not piece.done():
                piece.take()
    for copy in slot_copies:
        copy.wait_recv()
    for copy in slot_copies:
        copy.wait_send()
    for piece in pieces:
        piece.drain()


def learn(fields, pooled, lengths, dense, domains, cotangent, stats, model, field, counts, devices):
    w_in, tower_in, proj_w = model[4], model[11], model[0]
    experts, depth, units = w_in.shape
    width, events = dense.shape
    owners, _, cap = counts.shape
    tower_units = tower_in.shape[2]
    half = units // 2
    shape = Rows(experts, units, depth, tower_units, width)
    n_small = shape.padded(devices)
    blocks = [
        Block(depth, half, devices), Block(half, depth, devices),
        Block(DOMAINS * depth, tower_units, devices), Block(proj_w.shape[0], depth, devices),
    ]
    numbers = (2 * experts, 2 * experts, 1, 1)
    pieces = [(n, b.padded, b.lanes) for n, b in zip(numbers, blocks)]
    steps = 2 * (devices.bit_length() - 1)
    n_pieces = sum(numbers) + 1
    joined = proj_w.shape[0]
    space = lambda *s: pltpu.VMEM(s, f32)
    low = lambda *s: pltpu.VMEM(s, bf16)
    dma = lambda *s: pltpu.SemaphoreType.DMA(s)
    in_specs = [vmem()] * 24
    in_specs[11] = in_specs[13] = in_specs[23] = hbm()
    out = pl.pallas_call(
        functools.partial(learn_kernel, shape, blocks),
        in_specs=in_specs,
        out_specs=[vmem()] * 4 + [hbm()] * 5,
        out_shape=[
            jax.ShapeDtypeStruct((1, events), f32),
            jax.ShapeDtypeStruct((width, events), f32),
            jax.ShapeDtypeStruct((width, events), f32),
            jax.ShapeDtypeStruct((owners, width, cap), bf16),
            jax.ShapeDtypeStruct((n_small, 128), f32),
        ]
        + [jax.ShapeDtypeStruct(s, bf16) for s in pieces],
        scratch_shapes=[
            low(experts, depth, units), low(experts, units, depth), low(joined, events), low(events, joined),
            space(events, depth), space(events, depth), space(events, 1), low(events, depth),
            low(depth, events), space(events, 8), low(experts, events, units), low(experts, events, units),
            low(experts, events, depth), space(events, 8), space(events, depth), space(events, depth),
            low(events, depth), low(depth, events), low(DOMAINS, events, tower_units), space(events, depth),
            space(events, depth), space(events, 8), low(events, depth), low(events, units),
            low(joined - 2 * width, events), low(width, events), low(4, events, cap), space(owners * width, cap),
            low(owners, width, cap), space(n_small, 128), space(n_small, 128),
        ]
        + [pltpu.VMEM(s, bf16) for s in pieces] * 2
        + [space(n_small // devices, 128)]
        + [low(n, rows // devices, lanes) for n, rows, lanes in pieces]
        + [dma(experts), dma(experts), dma(4), dma(n_pieces), dma(n_pieces, steps), dma(n_pieces, steps), dma(devices), dma(devices)],
        compiler_params=params(collective_id=0, has_side_effects=True),
        name="learn",
    )(fields, pooled, lengths, dense, domains, cotangent, stats, *model, field, counts)
    return out[:5], [b.whole(t, n) for b, t, n in zip(blocks, out[5:], numbers)], shape


def get_row(small, at, n):
    return jnp.concatenate([small[at + c : at + c + 1, :] for c in range(n // 128)], axis=1)


def finish_kernel(shape, line, line_v, group, returned, domains, stats, centered, d_centered, small, *refs):
    more, out, more_out = refs[:4], refs[4], refs[5:9]
    d_dense, b_in, b_out, gain, bias, proj_b, inter_gain, inter_bias, gates, tower_in_bias, tower_out, tower_bias = refs[9:21]
    lines, vals = refs[21:]
    step = pl.program_id(0)
    per = out.shape[1] // ROW_CHUNK

    @pl.when(step == 0)
    def _():
        for target, places in (
            (b_in, shape.b_in), (b_out, shape.b_out), (gain, shape.gain), (bias, shape.bias),
            (proj_b, [shape.proj_b]), (inter_gain, [shape.inter_gain]), (inter_bias, [shape.inter_bias]),
            (gates, shape.gates), (tower_in_bias, shape.tower_in_bias), (tower_out, shape.tower_out),
            (tower_bias, [shape.tower_out_bias]),
        ):
            for i, at in enumerate(places):
                target[i : i + 1, :] = get_row(small, at, target.shape[1])
        which = domains[...]
        sums = small[shape.dense : shape.dense + centered.shape[0], :]
        moments = domain_moments(stats[...])
        scale = by_domain(which, [m[1] for m in moments])
        straight = by_domain(which, [sums[:, d : d + 1] / m[2] for d, m in enumerate(moments)])
        cross = by_domain(which, [sums[:, DOMAINS + d : DOMAINS + d + 1] / m[2] for d, m in enumerate(moments)])
        d_dense[...] = scale * (d_centered[...] - straight - centered[...] * cross)

        blocks, _, cap = group.shape

        def clear(i, carry):
            lines[pl.ds(pl.multiple_of(i * 1024, 1024), 1024), :] = jnp.zeros((1024, 128), f32)
            return carry

        lax.fori_loop(0, lines.shape[0] // 1024, clear, 0)
        batch = 32
        a = lax.div(lax.broadcasted_iota(i32, (cap, cap), 0), batch)
        near = a == lax.div(lax.broadcasted_iota(i32, (cap, cap), 1), batch)

        def serve(s, carry):
            which, own = group[s], returned[s].astype(f32)
            wide = jnp.concatenate([jnp.where(which == g, own, 0.0) for g in range(8)], axis=0)
            along = jnp.broadcast_to(line_v[s].astype(f32), (cap, cap))
            same = jnp.where(jnp.logical_and(along == along.T, near), 1.0, 0.0).astype(bf16)
            vals[...] = lax.dot_general(same, wide.astype(bf16), NT, preferred_element_type=f32)

            def add(u, carry):
                places, sums = [], []
                for k in range(batch):
                    j = u * batch + k
                    places.append(line[s * cap + j])
                    sums.append(lines[pl.ds(places[-1], 1), :] + vals[pl.ds(j, 1), :])
                for place, total in zip(places, sums):
                    lines[pl.ds(place, 1), :] = total
                return carry

            lax.fori_loop(0, cap // batch, add, 0)
            return carry

        lax.fori_loop(0, blocks, serve, 0)

    def turn(c, carry):
        width = out.shape[0]
        turned = lines[pl.ds(pl.multiple_of((step * per + c) * 128, 128), 128), :].T
        for g in range(8):
            at = pl.multiple_of(c * ROW_CHUNK + g * 128, 128)
            out[:, pl.ds(at, 128)] = turned[g * width : (g + 1) * width]
        return carry

    lax.fori_loop(0, per, turn, 0, unroll=4)
    for source, target in zip(more, more_out):
        tall, blocks, rows, lanes = source.shape
        for s in range(tall):
            for c in range(blocks):
                target[s * rows : (s + 1) * rows, c * lanes : (c + 1) * lanes] = source[s, c].astype(f32)


def finish(shape, line, group, returned, domains, stats, centered, d_centered, small, more, rows):
    blocks, width, cap = returned.shape
    events = centered.shape[1]
    experts, units, depth = len(shape.b_in), more[0].shape[1] * more[0].shape[3], more[0].shape[2]
    tower = more[2].shape[1] * more[2].shape[3]
    steps = 4
    in_more, out_more, shapes = [], [], []
    for x in more:
        tall, parts, r, lanes = x.shape
        if tall > 1:
            in_more.append(pl.BlockSpec((tall // steps, parts, r, lanes), lambda i: (i, 0, 0, 0)))
        else:
            in_more.append(pl.BlockSpec((1, parts, r // steps, lanes), lambda i: (0, 0, i, 0)))
        out_more.append(pl.BlockSpec((tall * r // steps, parts * lanes), lambda i: (i, 0)))
        shapes.append((tall * r, parts * lanes))
    shapes += [(width, events), (experts, units)] + [(experts, depth)] * 3 + [(1, depth)] * 3
    shapes += [(len(shape.gates), depth), (DOMAINS, tower), (DOMAINS, tower), (1, 128)]
    return pl.pallas_call(
        functools.partial(finish_kernel, shape),
        grid=(steps,),
        in_specs=[smem()] + [vmem()] * 8 + in_more,
        out_specs=[pl.BlockSpec((width, rows // steps), lambda i: (0, i))] + out_more + [vmem()] * 12,
        out_shape=[jax.ShapeDtypeStruct(s, f32) for s in [(width, rows)] + shapes],
        scratch_shapes=[pltpu.VMEM((rows // 8, 128), f32), pltpu.VMEM((cap, 128), f32)],
        compiler_params=params(),
        name="finish",
    )(line.reshape(-1), line, group, returned, domains, stats, centered, d_centered, small, *more)


def local(
    table,
    dense,
    domains,
    lengths,
    requests,
    counts,
    field_slots,
    behave_slots,
    proj_w,
    proj_b,
    inter_gain,
    inter_bias,
    w_in,
    b_in,
    w_out,
    b_out,
    expert_gain,
    expert_bias,
    shared_gate,
    group_gate,
    tower_in,
    tower_in_bias,
    tower_out,
    tower_out_bias,
    pred_cotangent,
):
    devices = lax.axis_size("wide") * lax.axis_size("narrow")
    capacity = requests.shape[2]
    experts, depth, units = w_in.shape
    starts = jnp.concatenate([jnp.zeros((1,), i32), jnp.cumsum(lengths.reshape(-1))])
    counts_of = slot_counts(starts, behave_slots.reshape(-1, 128), devices, capacity)
    field = field_slots.T
    dense_t, which = dense.T, domains[None]
    fields, pooled, line, group, stats = lookup(
        requests.reshape(devices, 1, capacity), table.T, counts.reshape(-1), field, counts_of, dense_t, which
    )
    gates = jnp.concatenate([shared_gate.T, group_gate.transpose(0, 2, 1).reshape(-1, depth)], axis=0)
    gates = jnp.pad(gates, ((0, GATE_ROWS - gates.shape[0]), (0, 0)))
    tall = lambda x: x.reshape(experts, 1, -1)
    model = (
        proj_w, proj_b[None], inter_gain[None], inter_bias[None], w_in, tall(b_in), w_out, tall(b_out),
        tall(expert_gain), tall(expert_bias), gates, tower_in, tower_in_bias, tower_out, tower_out_bias[None],
    )
    (pred, centered, d_centered, returned, small), totals, shape = learn(
        fields, pooled, lengths.astype(f32), dense_t, which, pred_cotangent[None], stats, model, field, counts_of, devices
    )
    totals[0] = totals[0].reshape(experts, -1, depth, totals[0].shape[3])
    out = finish(shape, line, group, returned, which, stats, centered, d_centered, small, totals, table.shape[0])
    d_table, d_w_in, d_w_out, d_tower_in, d_proj_w, d_dense, d_b_in, d_b_out, d_gain, d_bias = out[:10]
    d_proj_b, d_inter_gain, d_inter_bias, d_gates, d_tower_in_bias, d_tower_out, d_tower_bias = out[10:]
    return (
        pred[0],
        d_dense.T,
        d_table.T,
        d_proj_w,
        d_proj_b[0],
        d_inter_gain[0],
        d_inter_bias[0],
        d_w_in.reshape(w_in.shape),
        d_b_in,
        d_w_out.reshape(w_out.shape),
        d_b_out,
        d_gain,
        d_bias,
        d_gates[:SHARED].T,
        d_gates[SHARED:].reshape(DOMAINS, 2, depth).transpose(0, 2, 1),
        d_tower_in.reshape(tower_in.shape),
        d_tower_in_bias,
        d_tower_out,
        d_tower_bias[0, :DOMAINS],
    )


def solution(mesh):
    placed = (
        P(("wide", "narrow"), None),
        P(("wide", "narrow"), None),
        P(("wide", "narrow")),
        P(("wide", "narrow"), None),
        P(("wide", "narrow"), None, None),
        P(("wide", "narrow"), None),
        P(("wide", "narrow"), None),
        P(("wide", "narrow"), None),
        P(),
        P(),
        P(),
        P(),
        P(),
        P(),
        P(),
        P(),
        P(),
        P(),
        P(),
        P(),
        P(),
        P(),
        P(),
        P(),
        P(("wide", "narrow")),
    )
    return jax.shard_map(
        local,
        mesh=mesh,
        in_specs=placed,
        out_specs=(
            P(("wide", "narrow")),
            P(("wide", "narrow"), None),
            P(("wide", "narrow"), None),
            P(),
            P(),
            P(),
            P(),
            P(),
            P(),
            P(),
            P(),
            P(),
            P(),
            P(),
            P(),
            P(),
            P(),
            P(),
            P(),
        ),
        check_vma=False,
    )
```

time: 378 us -> 305 us (0.81); the launches traced: 372 us -> 304 us
  matrix products: 50.3 us -> 0 us
  Pallas kernels: 253 us -> 287 us
  local copies, waits for them, and re-layouts: 43.7 us -> 11.9 us
  other arithmetic: 23.5 us -> 4.32 us
    dot_general x42 -> x0, matrix products: 50.3 us -> none  [the longest x4 7.97 us: local(): jnp.einsum('ek,jk->ej', d_out_low, w_out[expert], preferred_element_type=...]
    pallas_call x3 -> x2, Pallas kernels: 167 us -> 202 us  [the longest x1 162 us: learn(): pl.pallas_call(functools.partial(learn_kernel, shape, blocks), in_specs=i...]
    unnamed x247 -> x3, local copies, waits for them, and re-layouts: 18.6 us -> 0.58 us
    reduce_sum x27 -> x0, other arithmetic: 10.9 us -> none  [the longest x8 4.13 us: layer_norm(): return center * lax.rsqrt(spread + EPSILON) * gain + shift]
    slice x14 -> x2, local copies, waits for them, and re-layouts: 10.8 us -> 0.79 us  [the longest x1 0.72 us: local(): d_gates[SHARED:].reshape(DOMAINS, 2, depth).transpose(0, 2, 1)]
where the time goes in v2:
time: 305 us; the launch traced here: 304 us
  Pallas kernels  287 us (94%)
  local copies, waits for them, and re-layouts  11.9 us (4%)
  other arithmetic  4.32 us (1%)
    pallas_call x1, Pallas kernels, learn(): pl.pallas_call(functools.partial(learn_kernel, shape, blocks), in_specs=i...  162 us
    pallas_call x1, Pallas kernels, lookup(): pl.pallas_call(lookup_kernel, in_specs=[vmem(), hbm(), smem(), vmem(), vm...  57.1 us
    pallas_call x1, Pallas kernels, finish(): pl.pallas_call(functools.partial(finish_kernel, shape), grid=(steps,), in...  40.3 us
    pallas_call x1, Pallas kernels, slot_counts(): pl.pallas_call(count_kernel, in_specs=[smem(), vmem()], out_specs=vmem(),...  27.7 us

profile of v2, /device:TPU:1, one launch (start us, length us, event | category | flops | bytes accessed | tf_op | source)
XLA Modules:
  0.0 304.1 jit_solution(8646272334088862901)
XLA Ops:
  0.7 1.0 reduce-window.9
  1.6 0.1 slice.16
  1.7 0.1 slice_reduce_fusion
  1.9 0.1 add_bitcast_fusion
  1.9 0.7 pad_add_fusion.starts
  2.6 1.3 convert_element_type.5.lengths
  3.9 0.7 reshape.111
  4.6 1.3 reshape.108.b_out
  5.9 1.3 reshape.109.expert_gain
  7.2 1.3 reshape.110.expert_bias
  8.5 1.3 fusion.2.gates
  9.8 1.3 reshape.107.b_in
  11.1 1.4 reshape.102.requests
  12.5 27.7 %slot_counts.1.counts.counts_hbm = bf16[32,512,256]{2,1,0:T(8,128)(2,1)} custom-call(s32[513]{0:T(1024)} %pad_add_fusion.starts, s32[256,128]{1,0:T(8,128)} %bitcast.42), custom_call_target="tpu_custom_call" | custom-call | tf_op jit(solution)/shard_map/slot_counts/pallas_call | solution.py:112
  40.2 57.1 %lookup.1 = (bf16[608,512]{1,0:T(8,128)(2,1)}, f32[16,512]{1,0:T(8,128)}, s32[32,1,256]{2,1,0:T(1,128)}, s32[32,1,256]{2,1,0:T(1,128)}, f32[16,128]{1,0:T(8,128)}) custom-call(s32[32,1,256]{2,1,0:T(1,128)} %reshape.102.requests, bf16[16,196608]{1,0:T(8,128)(2,1)} %bitcast.35, s32[32]{0:T(128)} %bitcast.58, s32[38,512]{1,0:T(8,128)} %bitcast.40, ...), custom_call_target="tpu_custom_call" | custom-call | tf_op jit(solution)/shard_map/lookup/pallas_call | solution.py:428
  97.3 162.1 %learn.1 = (f32[1,512]{1,0:T(1,128)}, f32[16,512]{1,0:T(8,128)}, f32[16,512]{1,0:T(8,128)}, bf16[32,16,256]{2,1,0:T(8,128)(2,1)}, f32[256,128]{1,0:T(8,128)}, /*...) custom-call(bf16[608,512]{1,0:T(8,128)(2,1)} %get-tuple-element.50.f, ...), custom_call_target="tpu_custom_call" | custom-call | tf_op jit(solution)/shard_map/learn/pallas_call | solution.py:872
  259.4 0.0 copy-start
  259.4 40.3 %finish.1 = (f32[16,196608]{1,0:T(8,128)}, f32[2048,1024]{1,0:T(8,128)}, f32[4096,512]{1,0:T(8,128)}, f32[1024,256]{1,0:T(8,128)}, f32[640,512]{1,0:T(8,128)}, /...) custom-call(s32[8192]{0:T(1024)} %bitcast.45, ...), custom_call_target="tpu_custom_call" | custom-call | tf_op jit(solution)/shard_map/finish/pallas_call | solution.py:999
  299.7 1.2 slice_bitcast_fusion.1
  300.9 1.3 slice_bitcast_fusion
  302.2 0.7 slice.19
  302.9 0.6 reshape.118
  303.5 0.0 copy-done
  303.6 0.6 copy.45
  (1 shorter events, 0.0 us)
Async XLA Ops:
  259.4 44.1 %copy-start = (f32[1,512]{1,0:T(1,128)S(1)}, f32[1,512]{1,0:T(1,128)}, u32[]{:S(2)}) copy-start(f32[1,512]{1,0:T(1,128)} %get-tuple-element.53) | copy-start | bytes 6148

commit v3 on v2

--- a/solution.py
+++ b/solution.py
@@ -24,6 +24,8 @@
 ROW_CHUNK = 1024
 GROUP = 8
 SPAN = 6
+BUNCH = 4
+ADD_STEPS = 4
 
 
 def vmem():
@@ -59,65 +61,69 @@
     return jnp.where(column == index, 1.0, 0.0).astype(bf16)
 
 
-def count_kernel(starts, behave, counts, sums):
-    owners, events, cap = counts.shape
+def count_kernel(lengths, behave, counts, sums, done):
+    owners, _, cap = counts.shape
     shift = cap.bit_length() - 1
+    step = pl.program_id(0)
     place = lax.broadcasted_iota(i32, (SPAN, 128), 0) * 128 + lax.broadcasted_iota(i32, (SPAN, 128), 1)
     last_block = behave.shape[0] - SPAN
-
-    def group(e0, k):
-        first, last = starts[e0], starts[e0 + GROUP]
-        cuts = [starts[e0 + i] for i in range(1, GROUP)]
-        b0 = lax.div(first, 128)
-
-        def part(m):
-            begin = b0 + m * SPAN
-            b = jnp.minimum(begin, last_block)
-            slot = behave[pl.ds(b, SPAN), :]
-            p = place + b * 128
-            event = jnp.zeros_like(p)
-            for cut in cuts:
-                event = event + jnp.where(p >= cut, 1, 0)
-            key = jnp.right_shift(slot, shift) * GROUP + event
-            mine = jnp.logical_and(jnp.logical_and(p >= first, p < last), p >= begin * 128)
-            key = jnp.where(mine, key, -1)
-            low = jnp.bitwise_and(slot, cap - 1)
-            left = jnp.concatenate([hot(owners * GROUP, key[q : q + 1]) for q in range(SPAN)], axis=1)
-            right = jnp.concatenate([hot(cap, low[q : q + 1]) for q in range(SPAN)], axis=1)
-            return lax.dot_general(left, right, NT, preferred_element_type=f32)
-
-        sums[k] = part(0)
-
-        def more(m, carry):
-            sums[k] += part(m)
-            return carry
-
-        lax.fori_loop(1, lax.div(last - b0 * 128 + (SPAN * 128 - 1), SPAN * 128), more, 0)
-
-    def pair(g, carry):
-        e0 = g * (2 * GROUP)
-        group(e0, 0)
-        group(e0 + GROUP, 1)
+    ends = [jnp.where(step == 0, 0, done[0])]
+    for i in range(BUNCH * GROUP):
+        ends.append(ends[-1] + lengths[0, step * (BUNCH * GROUP) + i])
+    done[0] = ends[-1]
+
+    def part(k, m):
+        cuts = ends[k * GROUP : (k + 1) * GROUP + 1]
+        begin = lax.div(cuts[0], 128) + m * SPAN
+        b = jnp.minimum(begin, last_block)
+        slot = behave[pl.ds(b, SPAN), :]
+        p = place + b * 128
+        event = jnp.zeros_like(p)
+        for cut in cuts[1:-1]:
+            event = event + jnp.where(p >= cut, 1, 0)
+        mine = jnp.logical_and(jnp.logical_and(p >= cuts[0], p < cuts[-1]), p >= begin * 128)
+        key = jnp.where(mine, jnp.right_shift(slot, shift) * GROUP + event, -1)
+        low = jnp.bitwise_and(slot, cap - 1)
+        left = jnp.concatenate([hot(owners * GROUP, key[q : q + 1]) for q in range(SPAN)], axis=1)
+        right = jnp.concatenate([hot(cap, low[q : q + 1]) for q in range(SPAN)], axis=1)
+        return lax.dot_general(left, right, NT, preferred_element_type=f32)
+
+    parts = []
+    for k in range(BUNCH):
+        sums[k] = part(k, 0)
+        first, last = ends[k * GROUP], ends[(k + 1) * GROUP]
+        parts.append(lax.div(last - lax.div(first, 128) * 128 + (SPAN * 128 - 1), SPAN * 128))
+    most = functools.reduce(jnp.maximum, parts)
+
+    @pl.when(most > 1)
+    def _():
+        for k in range(BUNCH):
+
+            def more(m, carry):
+                sums[k] += part(k, m)
+                return carry
+
+            lax.fori_loop(1, parts[k], more, 0)
+
+    for t in range(BUNCH // 2):
         for o in range(owners):
-            both = [sums[k, o * GROUP : (o + 1) * GROUP, :] for k in range(2)]
-            at = pl.ds(pl.multiple_of(e0, 2 * GROUP), 2 * GROUP)
-            counts[o, at, :] = jnp.concatenate(both, axis=0).astype(bf16)
-        return carry
-
-    lax.fori_loop(0, events // (2 * GROUP), pair, 0)
-
-
-def slot_counts(starts, behave, owners, cap):
-    events = starts.shape[0] - 1
+            both = [sums[2 * t + k, o * GROUP : (o + 1) * GROUP, :] for k in range(2)]
+            counts[o, t * 2 * GROUP : (t + 1) * 2 * GROUP, :] = jnp.concatenate(both, axis=0).astype(bf16)
+
+
+def slot_counts(lengths, behave, owners, cap):
+    events = lengths.shape[1]
+    size = BUNCH * GROUP
     return pl.pallas_call(
         count_kernel,
+        grid=(events // size,),
         in_specs=[smem(), vmem()],
-        out_specs=vmem(),
+        out_specs=pl.BlockSpec((owners, size, cap), lambda i: (0, i, 0)),
         out_shape=jax.ShapeDtypeStruct((owners, events, cap), bf16),
-        scratch_shapes=[pltpu.VMEM((2, owners * GROUP, cap), f32)],
+        scratch_shapes=[pltpu.VMEM((BUNCH, owners * GROUP, cap), f32), pltpu.SMEM((1,), i32)],
         compiler_params=params(),
         name="slot_counts",
-    )(starts, behave)
+    )(lengths, behave)
 
 
 def place_bits():
@@ -274,17 +280,16 @@
 
 
 def lookup_kernel(
-    requests, table, live, field, counts, dense, domains,
+    requests_in, table, live, field, counts_hbm, dense, domains,
     fields, pooled, line_out, group, stats_out,
-    tab, lines, got, line, line_smem, found, rows, slots, stats, stats_in,
-    tab_sems, line_sem, ask_sends, ask_recvs, row_sends, row_recvs, stat_sends, stat_recvs,
+    requests, counts, tab, lines, got, line, line_smem, found, rows, slots, stats, stats_in,
+    tab_sems, counts_sem, line_sem, ask_sends, ask_recvs, row_sends, row_recvs, stat_sends, stat_recvs,
 ):
     owners, _, cap = requests.shape
     width = tab.shape[0]
     n_field, events = field.shape
     chunks = tab_sems.shape[0]
     part = tab.shape[1] // chunks
-    batch = 4
     n_narrow = lax.axis_size("narrow")
     me = lax.axis_index("wide") * n_narrow + lax.axis_index("narrow")
 
@@ -293,6 +298,10 @@
         at = pl.ds(c * part, part)
         loads.append(pltpu.make_async_copy(table.at[:, at], tab.at[:, at], tab_sems.at[c]))
         loads[-1].start()
+    load_counts = pltpu.make_async_copy(counts_hbm, counts, counts_sem)
+    load_counts.start()
+    for o in range(owners):
+        requests[o] = requests_in[o : o + 1, :]
     lane = lax.broadcasted_iota(i32, (width, 128), 1)
     mine = jnp.zeros((width, 128), f32)
     for d in range(DOMAINS):
@@ -359,33 +368,34 @@
     to_smem.start()
     to_smem.wait()
 
-    def serve(b, carry):
-        sources = [lax.rem(me + b * batch + k, owners) for k in range(batch)]
-        for k in range(batch):
-
-            def fetch(u, carry):
-                for i in range(64):
-                    j = u * 64 + i
-                    got[pl.ds(k * cap + j, 1), :] = lines[pl.ds(line_smem[sources[k], 0, j], 1), :]
-                return carry
-
-            lax.fori_loop(0, cap // 64, fetch, 0)
-        turned = lax.dot_general(eye, got[...].astype(bf16), NT, preferred_element_type=f32)
-        for k in range(batch):
-            which = group[sources[k]]
-            picked = turned[:width, k * cap : (k + 1) * cap]
-            for g in range(1, 8):
-                picked = jnp.where(which == g, turned[g * width : (g + 1) * width, k * cap : (k + 1) * cap], picked)
-            found[sources[k]] = picked.astype(bf16)
-        for k in range(batch):
-            d = b * batch + k
-            if k:
-                answer(d).start()
-            else:
-                pl.when(b > 0)(lambda: answer(d).start())
+    def source(d):
+        return lax.rem(me + d, owners)
+
+    def fetch(d):
+        s, half = source(d), lax.rem(d, 2) * cap
+        for j in range(cap):
+            got[pl.ds(half + j, 1), :] = lines[pl.ds(line_smem[s, 0, j], 1), :]
+
+    def turn_out(d):
+        s, half = source(d), pl.multiple_of(lax.rem(d, 2) * cap, cap)
+        turned = lax.dot_general(eye, got[pl.ds(half, cap), :].astype(bf16), NT, preferred_element_type=f32)
+        which = jnp.broadcast_to(group[s], (width, cap))
+        picked = turned[:width]
+        for g in range(1, 8):
+            picked = jnp.where(which == g, turned[g * width : (g + 1) * width], picked)
+        found[s] = picked.astype(bf16)
+
+    fetch(0)
+
+    def serve(d, carry):
+        turn_out(d - 1)
+        fetch(d)
+        pl.when(d > 1)(lambda: answer(d - 1).start())
         return carry
 
-    lax.fori_loop(0, owners // batch, serve, 0)
+    lax.fori_loop(1, owners, serve, 0)
+    turn_out(owners - 1)
+    answer(owners - 1).start()
     rows[me] = found[me]
     each(1, lambda d: tell(d).wait_recv())
     total = stats_in[0]
@@ -401,7 +411,7 @@
 
     def one(f, carry):
         slot = field[pl.ds(f, 1), :]
-        owner = jnp.right_shift(slot, shift)
+        owner = jnp.broadcast_to(jnp.right_shift(slot, shift), (width, events))
         all_owners = jnp.dot(slots[...], hot(cap, jnp.bitwise_and(slot, cap - 1)), preferred_element_type=f32)
         picked = all_owners[:width]
         for o in range(1, owners):
@@ -410,6 +420,7 @@
         return carry
 
     lax.fori_loop(0, n_field, one, 0, unroll=2)
+    load_counts.wait()
     total = jnp.zeros((events, width), f32)
     for o in range(owners):
         total = total + lax.dot_general(counts[o], slots[o * width : (o + 1) * width, :], NT, preferred_element_type=f32)
@@ -420,14 +431,14 @@
 
 
 def lookup(requests, table_t, live, field_t, counts, dense_t, domains):
-    owners, _, cap = requests.shape
+    owners, cap = requests.shape
     width, rows = table_t.shape
     n_field, events = field_t.shape
     chunks = 6
     dma = pltpu.SemaphoreType.DMA
     return pl.pallas_call(
         lookup_kernel,
-        in_specs=[vmem(), hbm(), smem(), vmem(), vmem(), vmem(), vmem()],
+        in_specs=[vmem(), hbm(), smem(), vmem(), hbm(), vmem(), vmem()],
         out_specs=[vmem()] * 5,
         out_shape=[
             jax.ShapeDtypeStruct((n_field * width, events), bf16),
@@ -437,9 +448,11 @@
             jax.ShapeDtypeStruct((width, 128), f32),
         ],
         scratch_shapes=[
+            pltpu.VMEM((owners, 1, cap), i32),
+            pltpu.VMEM((owners, events, cap), bf16),
             pltpu.VMEM((width, rows), bf16),
             pltpu.VMEM((rows // 8, 128), f32),
-            pltpu.VMEM((4 * cap, 128), f32),
+            pltpu.VMEM((2 * cap, 128), f32),
             pltpu.VMEM((owners, 1, cap), i32),
             pltpu.SMEM((owners, 1, cap), i32),
             pltpu.VMEM((owners, width, cap), bf16),
@@ -448,6 +461,7 @@
             pltpu.VMEM((width, 128), f32),
             pltpu.VMEM((owners, width, 128), f32),
             dma((chunks,)),
+            dma,
             dma,
         ]
         + [dma((owners,))] * 6,
@@ -547,12 +561,12 @@
 def learn_kernel(
     shape, blocks,
     fields, pooled, lengths, dense, domains, cotangent, stats, proj_w, proj_b, inter_gain, inter_bias,
-    w_in_hbm, b_in, w_out_hbm, b_out, expert_gain, expert_bias, gates, tower_in, tower_in_bias, tower_out,
+    w_in_hbm, b_in, w_out_hbm, b_out, expert_gain, expert_bias, shared_gate, group_gate, tower_in, tower_in_bias, tower_out,
     tower_out_bias, field, counts_hbm,
     pred, centered, d_centered, returned, small_total, total_in, total_out, total_tower, total_proj,
-    w_in, w_out, joined, joined_rows, pre_slope, pre_standard, pre_inverse, state_low, state_turned, coef,
-    active, slope, standard, inverse, work, after, after_low, after_turned, d_tower, d_after, d_state, products,
-    d_out, d_in, d_fields, d_pooled, counts, slot_total, slot_grad,
+    w_in, w_out, joined, pre_slope, pre_standard, pre_inverse, state_low, state_turned, coef,
+    active, slope, standard, inverse, work, after, after_low, after_turned, d_tower, d_after, products,
+    d_out, d_in, d_pooled, gates, counts, slot_total, slot_grad,
     small_part, small_inbox, part_in, part_out, part_tower, part_proj, inbox_in, inbox_out, inbox_tower, inbox_proj,
     small_own, own_in, own_out, own_tower, own_proj, in_sems, out_sems, count_sems, own_sems, sends, recvs, slot_sends, slot_recvs,
 ):
@@ -567,12 +581,17 @@
         pltpu.make_async_copy(w_out_hbm.at[x], w_out.at[x], out_sems.at[x]).start()
 
     which = domains[...]
+    length = lengths[...].astype(f32)
+    rows = [shared_gate[...].astype(f32)] + [group_gate[d].astype(f32) for d in range(DOMAINS)]
+    have = SHARED + 2 * DOMAINS
+    gates[...] = jnp.concatenate(rows + [jnp.zeros((GATE_ROWS - have, depth), f32)], axis=0).astype(bf16)
     moments = domain_moments(stats[...])
     mean, scale = (by_domain(which, [m[i] for m in moments]) for i in range(2))
     centered[...] = (dense[...] - mean) * scale
     joined[: n_field * width, :] = fields[...]
-    joined[n_field * width : (n_field + 1) * width, :] = (pooled[...] / lengths[...]).astype(bf16)
+    joined[n_field * width : (n_field + 1) * width, :] = (pooled[...] / length).astype(bf16)
     joined[(n_field + 1) * width :, :] = centered[...].astype(bf16)
+    joined_rows, d_state, d_fields = d_in.at[:, : joined.shape[0]], after, joined
     joined_rows[...] = joined[...].T
     quarter = 256
 
@@ -617,7 +636,7 @@
 
         def enter(c):
             at = pl.ds(pl.multiple_of(c * quarter, quarter), quarter)
-            pre = jnp.dot(state_low[...], w_in[x, :, at], preferred_element_type=f32) + b_in[x, :, at]
+            pre = jnp.dot(state_low[...], w_in[x, :, at], preferred_element_type=f32) + b_in[x : x + 1, at]
             value, rise = gelu_and_slope(pre)
             active[x, :, at] = value.astype(bf16)
             slope[x, :, at] = rise.astype(bf16)
@@ -627,7 +646,7 @@
 
         def leave(c):
             at = pl.ds(pl.multiple_of(c * quarter, quarter), quarter)
-            work[:, at] = jnp.dot(active[x], w_out[x, :, at], preferred_element_type=f32) + b_out[x, :, at]
+            work[:, at] = jnp.dot(active[x], w_out[x, :, at], preferred_element_type=f32) + b_out[x : x + 1, at]
 
         loop(depth // quarter, leave)
 
@@ -635,7 +654,7 @@
             at = stripe(i)
             value, inverse[at, x : x + 1] = standardise(work[at, :])
             standard[x, at, :] = value.astype(bf16)
-            after[at, :] += coef[at, x : x + 1] * (value * expert_gain[x] + expert_bias[x])
+            after[at, :] += coef[at, x : x + 1] * (value * expert_gain[x : x + 1, :] + expert_bias[x : x + 1, :])
 
         loop(events // STRIPE, mix)
 
@@ -670,7 +689,14 @@
 
     wait_for_all()
     ways = orders()
-    pieces = []
+    pieces, clock = [], [0]
+
+    def pump():
+        for piece in pieces:
+            if not piece.done() and piece.sent_at < clock[0]:
+                piece.take()
+                piece.sent_at = clock[0]
+        clock[0] += 1
 
     def send(block, parts, inboxes, owns, totals, i, value):
         k = len(pieces)
@@ -679,6 +705,7 @@
             parts.at[i], inboxes.at[i], owns.at[i], totals.at[i], ways[k], own_sems.at[k], sends.at[k], recvs.at[k]
         )
         piece.send()
+        piece.sent_at = clock[0]
         pieces.append(piece)
 
     towers = [jnp.dot(after_turned[...], d_tower[d], preferred_element_type=f32).astype(bf16) for d in range(DOMAINS)]
@@ -696,9 +723,9 @@
         def unmix(i, sums):
             at = stripe(i)
             d, value = d_after[at, :], standard[x, at, :].astype(f32)
-            products[at, x : x + 1] = jnp.sum(d * (value * expert_gain[x] + expert_bias[x]), axis=1, keepdims=True)
+            products[at, x : x + 1] = jnp.sum(d * (value * expert_gain[x : x + 1, :] + expert_bias[x : x + 1, :]), axis=1, keepdims=True)
             d = coef[at, x : x + 1] * d
-            low = standardise_back(d * expert_gain[x], value, inverse[at, x : x + 1]).astype(bf16)
+            low = standardise_back(d * expert_gain[x : x + 1, :], value, inverse[at, x : x + 1]).astype(bf16)
             d_out[at, :] = low
             terms = (d * value, d, low.astype(f32))
             return tuple(s + jnp.sum(t, axis=0, keepdims=True) for s, t in zip(sums, terms))
@@ -706,7 +733,7 @@
         for place, row in zip((shape.gain[x], shape.bias[x], shape.b_out[x]),
                               lax.fori_loop(0, events // STRIPE, unmix, (zero,) * 3)):
             put_row(small_part, place, row)
-        older = list(pieces)
+        pump()
         for h in range(2):
             value = lax.dot_general(active[x, :, h * half : (h + 1) * half], d_out[...], TN, preferred_element_type=f32)
             send(blocks[1], part_out, inbox_out, own_out, total_out, 2 * x + h, value.astype(bf16))
@@ -730,8 +757,7 @@
             d_state[:, at] += lax.dot_general(d_in[...], w_in[x, at, :], NT, preferred_element_type=f32)
 
         loop(depth // quarter, unstate)
-        for piece in older:
-            piece.take()
+        pump()
 
     q = products[...].T
     q = [q[x : x + 1] for x in range(experts)]
@@ -772,9 +798,9 @@
     for o in range(ahead):
         fetch(o).start()
     n_all = n_field * width
-    d_fields[...] = lax.dot_general(proj_w[:n_all, :], d_out[...], NT, preferred_element_type=f32).astype(bf16)
+    d_fields[:n_all, :] = lax.dot_general(proj_w[:n_all, :], d_out[...], NT, preferred_element_type=f32).astype(bf16)
     tail = lax.dot_general(proj_w[n_all:, :], d_out[...], NT, preferred_element_type=f32)
-    d_pooled[...] = (tail[:width] / lengths[...]).astype(bf16)
+    d_pooled[...] = (tail[:width] / length).astype(bf16)
     d_centered[...] = tail[width:]
     lanes = lax.broadcasted_iota(i32, (width, 128), 1)
     sums = jnp.zeros((width, 128), f32)
@@ -790,9 +816,9 @@
         small_part, small_inbox, small_own, small_total, ways[0], own_sems.at[k], sends.at[k], recvs.at[k]
     )
     small_piece.send()
-    for piece in pieces:
-        piece.take()
+    small_piece.sent_at = clock[0]
     pieces.append(small_piece)
+    pump()
 
     shift = cap.bit_length() - 1
     slot_total[...] = jnp.zeros(slot_total.shape, f32)
@@ -807,14 +833,9 @@
         )
         return carry
 
-    def scatter_some(first, last):
-        lax.fori_loop(first, last, scatter, 0)
-
-    middle = n_field // 2
-    scatter_some(0, middle)
-    for piece in pieces:
-        piece.take()
-    scatter_some(middle, n_field)
+    for first in range(0, n_field, 4):
+        lax.fori_loop(first, min(first + 4, n_field), scatter, 0, unroll=2)
+        pump()
 
     def spread(o):
         fetch(o).wait()
@@ -823,7 +844,14 @@
         slot_grad[o] = (slot_total[at, :] + behave).astype(bf16)
         pl.when(o + ahead < owners)(lambda: fetch(o + ahead).start())
 
-    loop(owners, spread)
+    for first in range(0, owners, owners // 8):
+
+        def spread_some(o, carry):
+            spread(o)
+            return carry
+
+        lax.fori_loop(first, first + owners // 8, spread_some, 0)
+        pump()
     me = lax.axis_index("wide") * lax.axis_size("narrow") + lax.axis_index("narrow")
     slot_copies = []
     for d, other, place in everyone_else():
@@ -847,7 +875,7 @@
 
 
 def learn(fields, pooled, lengths, dense, domains, cotangent, stats, model, field, counts, devices):
-    w_in, tower_in, proj_w = model[4], model[11], model[0]
+    w_in, tower_in, proj_w = model[4], model[12], model[0]
     experts, depth, units = w_in.shape
     width, events = dense.shape
     owners, _, cap = counts.shape
@@ -867,8 +895,8 @@
     space = lambda *s: pltpu.VMEM(s, f32)
     low = lambda *s: pltpu.VMEM(s, bf16)
     dma = lambda *s: pltpu.SemaphoreType.DMA(s)
-    in_specs = [vmem()] * 24
-    in_specs[11] = in_specs[13] = in_specs[23] = hbm()
+    in_specs = [vmem()] * 25
+    in_specs[11] = in_specs[13] = in_specs[24] = hbm()
     out = pl.pallas_call(
         functools.partial(learn_kernel, shape, blocks),
         in_specs=in_specs,
@@ -882,13 +910,12 @@
         ]
         + [jax.ShapeDtypeStruct(s, bf16) for s in pieces],
         scratch_shapes=[
-            low(experts, depth, units), low(experts, units, depth), low(joined, events), low(events, joined),
+            low(experts, depth, units), low(experts, units, depth), low(joined, events),
             space(events, depth), space(events, depth), space(events, 1), low(events, depth),
             low(depth, events), space(events, 8), low(experts, events, units), low(experts, events, units),
             low(experts, events, depth), space(events, 8), space(events, depth), space(events, depth),
             low(events, depth), low(depth, events), low(DOMAINS, events, tower_units), space(events, depth),
-            space(events, depth), space(events, 8), low(events, depth), low(events, units),
-            low(joined - 2 * width, events), low(width, events), low(4, events, cap), space(owners * width, cap),
+            space(events, 8), low(events, depth), low(events, units), low(width, events), low(GATE_ROWS, depth), low(4, events, cap), space(owners * width, cap),
             low(owners, width, cap), space(n_small, 128), space(n_small, 128),
         ]
         + [pltpu.VMEM(s, bf16) for s in pieces] * 2
@@ -930,53 +957,65 @@
         cross = by_domain(which, [sums[:, DOMAINS + d : DOMAINS + d + 1] / m[2] for d, m in enumerate(moments)])
         d_dense[...] = scale * (d_centered[...] - straight - centered[...] * cross)
 
-        blocks, _, cap = group.shape
-
         def clear(i, carry):
             lines[pl.ds(pl.multiple_of(i * 1024, 1024), 1024), :] = jnp.zeros((1024, 128), f32)
             return carry
 
         lax.fori_loop(0, lines.shape[0] // 1024, clear, 0)
+
+    width, cap = returned.shape[1:]
+
+    @pl.when(step < ADD_STEPS)
+    def _():
         batch = 32
         a = lax.div(lax.broadcasted_iota(i32, (cap, cap), 0), batch)
         near = a == lax.div(lax.broadcasted_iota(i32, (cap, cap), 1), batch)
-
-        def serve(s, carry):
-            which, own = group[s], returned[s].astype(f32)
+        each = group.shape[0] // ADD_STEPS
+
+        def prepare(s, slot):
+            which, own = jnp.broadcast_to(group[s], (width, cap)), returned[s].astype(f32)
             wide = jnp.concatenate([jnp.where(which == g, own, 0.0) for g in range(8)], axis=0)
             along = jnp.broadcast_to(line_v[s].astype(f32), (cap, cap))
             same = jnp.where(jnp.logical_and(along == along.T, near), 1.0, 0.0).astype(bf16)
-            vals[...] = lax.dot_general(same, wide.astype(bf16), NT, preferred_element_type=f32)
-
-            def add(u, carry):
+            vals[slot] = lax.dot_general(same, wide.astype(bf16), NT, preferred_element_type=f32)
+
+        def add(s, slot):
+            for u in range(0, cap, batch):
                 places, sums = [], []
-                for k in range(batch):
-                    j = u * batch + k
+                for j in range(u, u + batch):
                     places.append(line[s * cap + j])
-                    sums.append(lines[pl.ds(places[-1], 1), :] + vals[pl.ds(j, 1), :])
+                    sums.append(lines[pl.ds(places[-1], 1), :] + vals[slot, j : j + 1, :])
                 for place, total in zip(places, sums):
                     lines[pl.ds(place, 1), :] = total
-                return carry
-
-            lax.fori_loop(0, cap // batch, add, 0)
+
+        prepare(step * each, 0)
+
+        def serve(i, carry):
+            s = step * each + i * 2
+            prepare(s + 1, 1)
+            add(s, 0)
+            prepare(jnp.minimum(s + 2, group.shape[0] - 1), 0)
+            add(s + 1, 1)
             return carry
 
-        lax.fori_loop(0, blocks, serve, 0)
-
-    def turn(c, carry):
-        width = out.shape[0]
-        turned = lines[pl.ds(pl.multiple_of((step * per + c) * 128, 128), 128), :].T
-        for g in range(8):
-            at = pl.multiple_of(c * ROW_CHUNK + g * 128, 128)
-            out[:, pl.ds(at, 128)] = turned[g * width : (g + 1) * width]
-        return carry
-
-    lax.fori_loop(0, per, turn, 0, unroll=4)
-    for source, target in zip(more, more_out):
-        tall, blocks, rows, lanes = source.shape
-        for s in range(tall):
-            for c in range(blocks):
-                target[s * rows : (s + 1) * rows, c * lanes : (c + 1) * lanes] = source[s, c].astype(f32)
+        lax.fori_loop(0, each // 2, serve, 0)
+        for source, target in zip(more, more_out):
+            tall, blocks, rows, lanes = source.shape
+            for s in range(tall):
+                for c in range(blocks):
+                    target[s * rows : (s + 1) * rows, c * lanes : (c + 1) * lanes] = source[s, c].astype(f32)
+
+    @pl.when(step >= ADD_STEPS)
+    def _():
+        def turn(c, carry):
+            at = pl.multiple_of(((step - ADD_STEPS) * per + c) * 128, 128)
+            turned = lines[pl.ds(at, 128), :].T
+            for g in range(8):
+                at = pl.multiple_of(c * ROW_CHUNK + g * 128, 128)
+                out[:, pl.ds(at, 128)] = turned[g * width : (g + 1) * width]
+            return carry
+
+        lax.fori_loop(0, per, turn, 0, unroll=4)
 
 
 def finish(shape, line, group, returned, domains, stats, centered, d_centered, small, more, rows):
@@ -984,25 +1023,26 @@
     events = centered.shape[1]
     experts, units, depth = len(shape.b_in), more[0].shape[1] * more[0].shape[3], more[0].shape[2]
     tower = more[2].shape[1] * more[2].shape[3]
-    steps = 4
+    steps, turns = ADD_STEPS, 4
+    early = lambda i: jnp.minimum(i, steps - 1)
     in_more, out_more, shapes = [], [], []
     for x in more:
         tall, parts, r, lanes = x.shape
         if tall > 1:
-            in_more.append(pl.BlockSpec((tall // steps, parts, r, lanes), lambda i: (i, 0, 0, 0)))
+            in_more.append(pl.BlockSpec((tall // steps, parts, r, lanes), lambda i: (early(i), 0, 0, 0)))
         else:
-            in_more.append(pl.BlockSpec((1, parts, r // steps, lanes), lambda i: (0, 0, i, 0)))
-        out_more.append(pl.BlockSpec((tall * r // steps, parts * lanes), lambda i: (i, 0)))
+            in_more.append(pl.BlockSpec((1, parts, r // steps, lanes), lambda i: (0, 0, early(i), 0)))
+        out_more.append(pl.BlockSpec((tall * r // steps, parts * lanes), lambda i: (early(i), 0)))
         shapes.append((tall * r, parts * lanes))
     shapes += [(width, events), (experts, units)] + [(experts, depth)] * 3 + [(1, depth)] * 3
     shapes += [(len(shape.gates), depth), (DOMAINS, tower), (DOMAINS, tower), (1, 128)]
     return pl.pallas_call(
         functools.partial(finish_kernel, shape),
-        grid=(steps,),
+        grid=(steps + turns,),
         in_specs=[smem()] + [vmem()] * 8 + in_more,
-        out_specs=[pl.BlockSpec((width, rows // steps), lambda i: (0, i))] + out_more + [vmem()] * 12,
+        out_specs=[pl.BlockSpec((width, rows // turns), lambda i: (0, jnp.maximum(i - steps, 0)))] + out_more + [vmem()] * 12,
         out_shape=[jax.ShapeDtypeStruct(s, f32) for s in [(width, rows)] + shapes],
-        scratch_shapes=[pltpu.VMEM((rows // 8, 128), f32), pltpu.VMEM((cap, 128), f32)],
+        scratch_shapes=[pltpu.VMEM((rows // 8, 128), f32), pltpu.VMEM((2, cap, 128), f32)],
         compiler_params=params(),
         name="finish",
     )(line.reshape(-1), line, group, returned, domains, stats, centered, d_centered, small, *more)
@@ -1038,22 +1078,18 @@
     devices = lax.axis_size("wide") * lax.axis_size("narrow")
     capacity = requests.shape[2]
     experts, depth, units = w_in.shape
-    starts = jnp.concatenate([jnp.zeros((1,), i32), jnp.cumsum(lengths.reshape(-1))])
-    counts_of = slot_counts(starts, behave_slots.reshape(-1, 128), devices, capacity)
+    counts_of = slot_counts(lengths, behave_slots.reshape(-1, 128), devices, capacity)
     field = field_slots.T
     dense_t, which = dense.T, domains[None]
     fields, pooled, line, group, stats = lookup(
-        requests.reshape(devices, 1, capacity), table.T, counts.reshape(-1), field, counts_of, dense_t, which
+        requests[0], table.T, counts.reshape(-1), field, counts_of, dense_t, which
     )
-    gates = jnp.concatenate([shared_gate.T, group_gate.transpose(0, 2, 1).reshape(-1, depth)], axis=0)
-    gates = jnp.pad(gates, ((0, GATE_ROWS - gates.shape[0]), (0, 0)))
-    tall = lambda x: x.reshape(experts, 1, -1)
     model = (
-        proj_w, proj_b[None], inter_gain[None], inter_bias[None], w_in, tall(b_in), w_out, tall(b_out),
-        tall(expert_gain), tall(expert_bias), gates, tower_in, tower_in_bias, tower_out, tower_out_bias[None],
+        proj_w, proj_b[None], inter_gain[None], inter_bias[None], w_in, b_in, w_out, b_out, expert_gain, expert_bias,
+        shared_gate.T, group_gate.transpose(0, 2, 1), tower_in, tower_in_bias, tower_out, tower_out_bias[None],
     )
     (pred, centered, d_centered, returned, small), totals, shape = learn(
-        fields, pooled, lengths.astype(f32), dense_t, which, pred_cotangent[None], stats, model, field, counts_of, devices
+        fields, pooled, lengths, dense_t, which, pred_cotangent[None], stats, model, field, counts_of, devices
     )
     totals[0] = totals[0].reshape(experts, -1, depth, totals[0].shape[3])
     out = finish(shape, line, group, returned, which, stats, centered, d_centered, small, totals, table.shape[0])

time: 305 us -> 257 us (0.84)
  Pallas kernels: 287 us -> 251 us
  local copies, waits for them, and re-layouts: 11.9 us -> 4.4 us
  other arithmetic: 4.32 us -> 0 us
    pallas_call x3, Pallas kernels: 125 us -> 86.4 us  [the longest x1 40.6 us: lookup(): pl.pallas_call(lookup_kernel, in_specs=[vmem(), hbm(), smem(), vmem(), hb...]
    reshape x6 -> x0, local copies, waits for them, and re-layouts: 7.32 us -> none  [the longest x4 5.23 us: local(): tall = lambda x: x.reshape(experts, 1, -1)]
where the time goes in v3:
time: 257 us; the launch traced here: 256 us
  Pallas kernels  251 us (98%)
  local copies, waits for them, and re-layouts  4.4 us (2%)
    pallas_call x1, Pallas kernels, learn(): pl.pallas_call(functools.partial(learn_kernel, shape, blocks), in_specs=i...  164 us
    pallas_call x1, Pallas kernels, lookup(): pl.pallas_call(lookup_kernel, in_specs=[vmem(), hbm(), smem(), vmem(), hb...  40.6 us
    pallas_call x1, Pallas kernels, finish(): pl.pallas_call(functools.partial(finish_kernel, shape), grid=(steps + tur...  28.3 us
    pallas_call x1, Pallas kernels, slot_counts(): pl.pallas_call(count_kernel, grid=(events // size,), in_specs=[smem(), vm...  17.6 us

profile of v3, /device:TPU:1, one launch (start us, length us, event | category | flops | bytes accessed | tf_op | source)
XLA Modules:
  0.0 255.7 jit_solution(4403690016317676749)
XLA Ops:
  0.7 17.6 %slot_counts.1.counts_hbm = bf16[32,512,256]{2,1,0:T(8,128)(2,1)} custom-call(s32[1,512]{1,0:T(1,128)} %lengths.3, s32[256,128]{1,0:T(8,128)} %bitcast.40), custom_call_target="tpu_custom_call" | custom-call | tf_op jit(solution)/shard_map/slot_counts/pallas_call | solution.py:117
  18.2 40.6 %lookup.1 = (bf16[608,512]{1,0:T(8,128)(2,1)}, f32[16,512]{1,0:T(8,128)}, s32[32,1,256]{2,1,0:T(1,128)}, s32[32,1,256]{2,1,0:T(1,128)}, f32[16,128]{1,0:T(8,128)}) custom-call(s32[32,256]{1,0:T(8,128)} %bitcast.44, bf16[16,196608]{1,0:T(8,128)(2,1)} %bitcast.33, s32[32]{0:T(128)} %bitcast.56, s32[38,512]{1,0:T(8,128)} %bitcast.38, ...), custom_call_target="tpu_custom_call" | custom-call | tf_op jit(solution)/shard_map/lookup/pallas_call | solution.py:439
  58.8 164.2 %learn.1 = (f32[1,512]{1,0:T(1,128)}, f32[16,512]{1,0:T(8,128)}, f32[16,512]{1,0:T(8,128)}, bf16[32,16,256]{2,1,0:T(8,128)(2,1)}, f32[256,128]{1,0:T(8,128)}, /*...) custom-call(bf16[608,512]{1,0:T(8,128)(2,1)} %get-tuple-element.50.f, ...), custom_call_target="tpu_custom_call" | custom-call | tf_op jit(solution)/shard_map/learn/pallas_call | solution.py:900
  223.0 0.0 copy-start
  223.0 28.3 %finish.1 = (f32[16,196608]{1,0:T(8,128)}, f32[2048,1024]{1,0:T(8,128)}, f32[4096,512]{1,0:T(8,128)}, f32[1024,256]{1,0:T(8,128)}, f32[640,512]{1,0:T(8,128)}, /...) custom-call(s32[8192]{0:T(1024)} %bitcast.43, ...), custom_call_target="tpu_custom_call" | custom-call | tf_op jit(solution)/shard_map/finish/pallas_call | solution.py:1039
  251.3 1.2 slice_bitcast_fusion.1
  252.5 1.3 slice_bitcast_fusion
  253.8 0.7 slice.10
  254.5 0.6 reshape.76
  255.1 0.0 copy-done
  255.1 0.6 copy.45
Async XLA Ops:
  223.0 32.1 %copy-start = (f32[1,512]{1,0:T(1,128)S(1)}, f32[1,512]{1,0:T(1,128)}, u32[]{:S(2)}) copy-start(f32[1,512]{1,0:T(1,128)} %get-tuple-element.53) | copy-start | bytes 6148

commit v4 on v3

--- a/solution.py
+++ b/solution.py
@@ -245,7 +245,7 @@
     return lanes
 
 
-ORDERS = "BDADABGGBBBABGBAAA"
+ORDERS = "ABABGABDABABGABABA"
 
 
 class Block:
@@ -470,7 +470,7 @@
     )(requests, table_t, live, field_t, counts, dense_t, domains)
 
 
-STRIPE = 64
+STRIPE = 128
 GATE_ROWS = 16
 GELU_SCALE = math.sqrt(2.0 / math.pi)
 GELU_CUBE = 0.044715
@@ -499,7 +499,7 @@
         body(i)
         return carry
 
-    lax.fori_loop(0, n, step, 0)
+    lax.fori_loop(0, n, step, 0, unroll=2)
 
 
 def columns(rows):
@@ -693,7 +693,7 @@
 
     def pump():
         for piece in pieces:
-            if not piece.done() and piece.sent_at < clock[0]:
+            if not piece.done() and piece.sent_at < clock[0] - 2:
                 piece.take()
                 piece.sent_at = clock[0]
         clock[0] += 1
@@ -731,7 +731,7 @@
             return tuple(s + jnp.sum(t, axis=0, keepdims=True) for s, t in zip(sums, terms))
 
         for place, row in zip((shape.gain[x], shape.bias[x], shape.b_out[x]),
-                              lax.fori_loop(0, events // STRIPE, unmix, (zero,) * 3)):
+                              lax.fori_loop(0, events // STRIPE, unmix, (zero,) * 3, unroll=2)):
             put_row(small_part, place, row)
         pump()
         for h in range(2):
@@ -759,6 +759,14 @@
         loop(depth // quarter, unstate)
         pump()
 
+    ahead = counts.shape[0]
+
+    def fetch(o):
+        slot = o % ahead if isinstance(o, int) else lax.rem(o, ahead)
+        return pltpu.make_async_copy(counts_hbm.at[o], counts.at[slot], count_sems.at[slot])
+
+    for o in range(ahead):
+        fetch(o).start()
     q = products[...].T
     q = [q[x : x + 1] for x in range(experts)]
     d_level = (share[0] * q[0] + share[1] * q[1], by_domain(which, q[SHARED:]))
@@ -785,18 +793,10 @@
         return tuple(s + jnp.sum(t, axis=0, keepdims=True) for s, t in zip(sums, terms))
 
     for place, row in zip((shape.inter_gain, shape.inter_bias, shape.proj_b),
-                          lax.fori_loop(0, events // STRIPE, unstart, (zero,) * 3)):
+                          lax.fori_loop(0, events // STRIPE, unstart, (zero,) * 3, unroll=2)):
         put_row(small_part, place, row)
     value = jnp.dot(joined[...], d_out[...], preferred_element_type=f32)
     send(blocks[3], part_proj, inbox_proj, own_proj, total_proj, 0, value.astype(bf16))
-    ahead = counts.shape[0]
-
-    def fetch(o):
-        slot = o % ahead if isinstance(o, int) else lax.rem(o, ahead)
-        return pltpu.make_async_copy(counts_hbm.at[o], counts.at[slot], count_sems.at[slot])
-
-    for o in range(ahead):
-        fetch(o).start()
     n_all = n_field * width
     d_fields[:n_all, :] = lax.dot_general(proj_w[:n_all, :], d_out[...], NT, preferred_element_type=f32).astype(bf16)
     tail = lax.dot_general(proj_w[n_all:, :], d_out[...], NT, preferred_element_type=f32)
@@ -824,17 +824,22 @@
     slot_total[...] = jnp.zeros(slot_total.shape, f32)
 
     def scatter(f, carry):
-        slot = field[pl.ds(f, 1), :]
-        owner = jnp.right_shift(slot, shift)
-        d = d_fields[pl.ds(pl.multiple_of(f * width, width), width), :].astype(f32)
-        wide = jnp.concatenate([jnp.where(owner == o, d, 0.0).astype(bf16) for o in range(owners)], axis=0)
+        wide, hots = [], []
+        for k in range(2):
+            slot = field[pl.ds(f * 2 + k, 1), :]
+            owner = jnp.broadcast_to(jnp.right_shift(slot, shift), (width, events))
+            d = d_fields[pl.ds(pl.multiple_of((f * 2 + k) * width, width), width), :].astype(f32)
+            wide.append(
+                jnp.concatenate([jnp.where(owner == o, d, 0.0).astype(bf16) for o in range(owners)], axis=0)
+            )
+            hots.append(hot(cap, jnp.bitwise_and(slot, cap - 1)))
         slot_total[...] += lax.dot_general(
-            wide, hot(cap, jnp.bitwise_and(slot, cap - 1)), NT, preferred_element_type=f32
+            jnp.concatenate(wide, axis=1), jnp.concatenate(hots, axis=1), NT, preferred_element_type=f32
         )
         return carry
 
-    for first in range(0, n_field, 4):
-        lax.fori_loop(first, min(first + 4, n_field), scatter, 0, unroll=2)
+    for first in range(0, n_field // 2, 2):
+        lax.fori_loop(first, min(first + 2, n_field // 2), scatter, 0)
         pump()
 
     def spread(o):
@@ -892,6 +897,7 @@
     steps = 2 * (devices.bit_length() - 1)
     n_pieces = sum(numbers) + 1
     joined = proj_w.shape[0]
+    ahead = max(4, min(16, 512 // devices))
     space = lambda *s: pltpu.VMEM(s, f32)
     low = lambda *s: pltpu.VMEM(s, bf16)
     dma = lambda *s: pltpu.SemaphoreType.DMA(s)
@@ -915,13 +921,13 @@
             low(depth, events), space(events, 8), low(experts, events, units), low(experts, events, units),
             low(experts, events, depth), space(events, 8), space(events, depth), space(events, depth),
             low(events, depth), low(depth, events), low(DOMAINS, events, tower_units), space(events, depth),
-            space(events, 8), low(events, depth), low(events, units), low(width, events), low(GATE_ROWS, depth), low(4, events, cap), space(owners * width, cap),
+            space(events, 8), low(events, depth), low(events, units), low(width, events), low(GATE_ROWS, depth), low(ahead, events, cap), space(owners * width, cap),
             low(owners, width, cap), space(n_small, 128), space(n_small, 128),
         ]
         + [pltpu.VMEM(s, bf16) for s in pieces] * 2
         + [space(n_small // devices, 128)]
         + [low(n, rows // devices, lanes) for n, rows, lanes in pieces]
-        + [dma(experts), dma(experts), dma(4), dma(n_pieces), dma(n_pieces, steps), dma(n_pieces, steps), dma(devices), dma(devices)],
+        + [dma(experts), dma(experts), dma(ahead), dma(n_pieces), dma(n_pieces, steps), dma(n_pieces, steps), dma(devices), dma(devices)],
         compiler_params=params(collective_id=0, has_side_effects=True),
         name="learn",
     )(fields, pooled, lengths, dense, domains, cotangent, stats, *model, field, counts)
@@ -934,8 +940,8 @@
 
 def finish_kernel(shape, line, line_v, group, returned, domains, stats, centered, d_centered, small, *refs):
     more, out, more_out = refs[:4], refs[4], refs[5:9]
-    d_dense, b_in, b_out, gain, bias, proj_b, inter_gain, inter_bias, gates, tower_in_bias, tower_out, tower_bias = refs[9:21]
-    lines, vals = refs[21:]
+    d_dense, b_in, b_out, gain, bias, proj_b, inter_gain, inter_bias, shared_gate, group_gate, tower_in_bias, tower_out, tower_bias = refs[9:22]
+    lines, vals = refs[22:]
     step = pl.program_id(0)
     per = out.shape[1] // ROW_CHUNK
 
@@ -944,11 +950,13 @@
         for target, places in (
             (b_in, shape.b_in), (b_out, shape.b_out), (gain, shape.gain), (bias, shape.bias),
             (proj_b, [shape.proj_b]), (inter_gain, [shape.inter_gain]), (inter_bias, [shape.inter_bias]),
-            (gates, shape.gates), (tower_in_bias, shape.tower_in_bias), (tower_out, shape.tower_out),
-            (tower_bias, [shape.tower_out_bias]),
+            (shared_gate, shape.gates[:SHARED]), (tower_in_bias, shape.tower_in_bias), (tower_out, shape.tower_out),
         ):
             for i, at in enumerate(places):
                 target[i : i + 1, :] = get_row(small, at, target.shape[1])
+        for i, at in enumerate(shape.gates[SHARED:]):
+            group_gate[i // 2, i % 2 : i % 2 + 1, :] = get_row(small, at, group_gate.shape[2])
+        tower_bias[...] = small[shape.tower_out_bias : shape.tower_out_bias + 1, : tower_bias.shape[1]]
         which = domains[...]
         sums = small[shape.dense : shape.dense + centered.shape[0], :]
         moments = domain_moments(stats[...])
@@ -1035,12 +1043,12 @@
         out_more.append(pl.BlockSpec((tall * r // steps, parts * lanes), lambda i: (early(i), 0)))
         shapes.append((tall * r, parts * lanes))
     shapes += [(width, events), (experts, units)] + [(experts, depth)] * 3 + [(1, depth)] * 3
-    shapes += [(len(shape.gates), depth), (DOMAINS, tower), (DOMAINS, tower), (1, 128)]
+    shapes += [(SHARED, depth), (DOMAINS, 2, depth), (DOMAINS, tower), (DOMAINS, tower), (1, DOMAINS)]
     return pl.pallas_call(
         functools.partial(finish_kernel, shape),
         grid=(steps + turns,),
         in_specs=[smem()] + [vmem()] * 8 + in_more,
-        out_specs=[pl.BlockSpec((width, rows // turns), lambda i: (0, jnp.maximum(i - steps, 0)))] + out_more + [vmem()] * 12,
+        out_specs=[pl.BlockSpec((width, rows // turns), lambda i: (0, jnp.maximum(i - steps, 0)))] + out_more + [vmem()] * 13,
         out_shape=[jax.ShapeDtypeStruct(s, f32) for s in [(width, rows)] + shapes],
         scratch_shapes=[pltpu.VMEM((rows // 8, 128), f32), pltpu.VMEM((2, cap, 128), f32)],
         compiler_params=params(),
@@ -1094,7 +1102,7 @@
     totals[0] = totals[0].reshape(experts, -1, depth, totals[0].shape[3])
     out = finish(shape, line, group, returned, which, stats, centered, d_centered, small, totals, table.shape[0])
     d_table, d_w_in, d_w_out, d_tower_in, d_proj_w, d_dense, d_b_in, d_b_out, d_gain, d_bias = out[:10]
-    d_proj_b, d_inter_gain, d_inter_bias, d_gates, d_tower_in_bias, d_tower_out, d_tower_bias = out[10:]
+    d_proj_b, d_inter_gain, d_inter_bias, d_shared_gate, d_group_gate, d_tower_in_bias, d_tower_out, d_tower_bias = out[10:]
     return (
         pred[0],
         d_dense.T,
@@ -1109,12 +1117,12 @@
         d_b_out,
         d_gain,
         d_bias,
-        d_gates[:SHARED].T,
-        d_gates[SHARED:].reshape(DOMAINS, 2, depth).transpose(0, 2, 1),
+        d_shared_gate.T,
+        d_group_gate.transpose(0, 2, 1),
         d_tower_in.reshape(tower_in.shape),
         d_tower_in_bias,
         d_tower_out,
-        d_tower_bias[0, :DOMAINS],
+        d_tower_bias[0],
     )
 
 

time: 257 us -> 229 us (0.89)
  Pallas kernels: 251 us -> 224 us
  local copies, waits for them, and re-layouts: 4.4 us -> 0.58 us
    pallas_call x1, Pallas kernels: 164 us -> 137 us  [learn(): pl.pallas_call(functools.partial(learn_kernel, shape, blocks), in_specs=i...]
where the time goes in v4:
time: 229 us; the launch traced here: 225 us
  Pallas kernels  224 us (98%)
    pallas_call x1, Pallas kernels, learn(): pl.pallas_call(functools.partial(learn_kernel, shape, blocks), in_specs=i...  137 us
    pallas_call x1, Pallas kernels, lookup(): pl.pallas_call(lookup_kernel, in_specs=[vmem(), hbm(), smem(), vmem(), hb...  40.3 us
    pallas_call x1, Pallas kernels, finish(): pl.pallas_call(functools.partial(finish_kernel, shape), grid=(steps + tur...  28.3 us
    pallas_call x1, Pallas kernels, slot_counts(): pl.pallas_call(count_kernel, grid=(events // size,), in_specs=[smem(), vm...  17.9 us

profile of v4, /device:TPU:1, one launch (start us, length us, event | category | flops | bytes accessed | tf_op | source)
XLA Modules:
  0.0 225.2 jit_solution(6348853406036394598)
XLA Ops:
  0.7 17.9 %slot_counts.1.counts_hbm = bf16[32,512,256]{2,1,0:T(8,128)(2,1)} custom-call(s32[1,512]{1,0:T(1,128)} %lengths.3, s32[256,128]{1,0:T(8,128)} %bitcast.38), custom_call_target="tpu_custom_call" | custom-call | tf_op jit(solution)/shard_map/slot_counts/pallas_call | solution.py:117
  18.5 40.3 %lookup.1 = (bf16[608,512]{1,0:T(8,128)(2,1)}, f32[16,512]{1,0:T(8,128)}, s32[32,1,256]{2,1,0:T(1,128)}, s32[32,1,256]{2,1,0:T(1,128)}, f32[16,128]{1,0:T(8,128)}) custom-call(s32[32,256]{1,0:T(8,128)} %bitcast.42, bf16[16,196608]{1,0:T(8,128)(2,1)} %bitcast.31, s32[32]{0:T(128)} %bitcast.53, s32[38,512]{1,0:T(8,128)} %bitcast.36, ...), custom_call_target="tpu_custom_call" | custom-call | tf_op jit(solution)/shard_map/lookup/pallas_call | solution.py:439
  58.8 137.3 %learn.1 = (f32[1,512]{1,0:T(1,128)}, f32[16,512]{1,0:T(8,128)}, f32[16,512]{1,0:T(8,128)}, bf16[32,16,256]{2,1,0:T(8,128)(2,1)}, f32[256,128]{1,0:T(8,128)}, /*...) custom-call(bf16[608,512]{1,0:T(8,128)(2,1)} %get-tuple-element.51.f, ...), custom_call_target="tpu_custom_call" | custom-call | tf_op jit(solution)/shard_map/learn/pallas_call | solution.py:906
  196.1 0.0 copy-start
  196.1 28.3 %finish.1 = (f32[16,196608]{1,0:T(8,128)}, f32[2048,1024]{1,0:T(8,128)}, f32[4096,512]{1,0:T(8,128)}, f32[1024,256]{1,0:T(8,128)}, f32[640,512]{1,0:T(8,128)}, /...) custom-call(s32[8192]{0:T(1024)} %bitcast.41, ...), custom_call_target="tpu_custom_call" | custom-call | tf_op jit(solution)/shard_map/finish/pallas_call | solution.py:1047
  224.4 0.0 copy-done
  224.4 0.6 copy.45
Async XLA Ops:
  196.1 28.3 %copy-start = (f32[1,512]{1,0:T(1,128)S(1)}, f32[1,512]{1,0:T(1,128)}, u32[]{:S(2)}) copy-start(f32[1,512]{1,0:T(1,128)} %get-tuple-element.54) | copy-start | bytes 6148
